TPU v7x, 32 devices: a whole 2x2x4 slice. The times are simulated.
32 devices in a mesh: frame: 4 (over y, x), head: 4 (over z), tok: 2 (over core).
Axes of the slice: x: 2, y: 2, z: 4, core: 2. Of those that a mesh axis runs over, the one named last changes fastest.
Arguments:
- queries: bfloat16 [4, 768, 512], P('frame', ('head', 'tok')), may hold values from -120 to 120
- keys: bfloat16 [4, 768, 512], P('frame', ('head', 'tok')), may hold values from -4 to 4
- values: bfloat16 [4, 768, 512], P('frame', ('head', 'tok')), may hold values from -6 to 6
- residual: bfloat16 [4, 768, 512], P('frame', ('head', 'tok')), may hold values from -6 to 6
- incoming: bfloat16 [768, 512], P(('head', 'tok')), may hold values from -6 to 6
- gate_table: float32 [50, 512], replicated, may hold values from -2 to 2
- timesteps: int32 [4], P('frame'), may hold values from 0 to 49
- positions: int32 [4], P('frame'), may hold values from 0 to 9, as said below
Outputs:
- next_queue: bfloat16 [4, 768, 512], P('frame', ('head', 'tok'))
- leaving: bfloat16 [768, 512], P(('head', 'tok'), 'frame')
Inputs may be any that keep to these rules, and one draw needn't show every extreme that they name: positions rise strictly along the queue, by 1 to 5 from one frame to the next; the first frame's position is 0 and the last frame's is 9.
All inputs are finite; a program needn't handle non-finite values.
Results may differ from a plain program's by a relative error of at most 0.007.
Values may be sent and summed in bfloat16 or wider, within the bound.
A program may use at most 64 MiB of HBM per device.

v0:
```python
import math

import jax
import jax.numpy as jnp
from jax import lax
from jax.sharding import PartitionSpec as P

HD = 128
ROPE_DIMS = 16


rope_base = 256.0


def shifted(block, axis, distance):
    devices = range(lax.axis_size(axis))
    route = [(i - distance, i) for i in devices if i - distance in devices]
    return lax.ppermute(block, axis, route)


def from_root(block, axis, source):
    block = jnp.where(lax.axis_index(axis) == source, block, jnp.zeros_like(block))
    return lax.psum(block, axis)


def rotate(block_data, positions):
    frames, tokens, columns_all = block_data.shape
    shaped = block_data.astype(jnp.float32).reshape(frames, tokens, columns_all // HD, HD)
    half_dims = ROPE_DIMS // 2
    frequency = rope_base ** (-jnp.arange(half_dims, dtype=jnp.float32) / half_dims)
    angles = positions.astype(jnp.float32)[:, None, None, None] * frequency
    cosine = jnp.cos(angles)
    sine_term = jnp.sin(angles)
    leading = shaped[..., :half_dims]
    second = shaped[..., half_dims:ROPE_DIMS]
    turned = jnp.concatenate(
        [
            leading * cosine - second * sine_term,
            second * cosine + leading * sine_term,
            shaped[..., ROPE_DIMS:],
        ],
        axis=-1,
    )
    return turned.reshape(frames, tokens, columns_all).astype(jnp.bfloat16)


def block_stats(query_rows, block_keys, block_values, usable, score_scale):
    scores = (
        jnp.einsum("qd,kd->qk", query_rows, block_keys, preferred_element_type=jnp.float32)
        * score_scale
    )
    highest = jnp.max(scores, axis=1, keepdims=True)
    weights = jnp.where(usable, jnp.exp(scores - highest), 0.0)
    running_total = jnp.sum(weights, axis=1, keepdims=True)
    blended = jnp.dot(
        weights.astype(jnp.bfloat16), block_values, preferred_element_type=jnp.float32
    )
    return (jnp.where(usable, highest, -1e30), running_total, blended)


def attend(query_rows, key_blocks, score_scale):
    partials = [
        block_stats(query_rows, block_keys, block_values, usable, score_scale)
        for block_keys, block_values, usable in key_blocks
    ]
    summit = partials[0][0]
    for entry in partials[1:]:
        summit = jnp.maximum(summit, entry[0])
    running_total = jnp.zeros_like(summit)
    blended = jnp.zeros((query_rows.shape[0], HD), jnp.float32)
    for entry in partials:
        factor = jnp.exp(entry[0] - summit)
        running_total = running_total + factor * entry[1]
        blended = blended + factor * entry[2]
    return (blended / running_total).astype(jnp.bfloat16)


def per_device(queries, keys, values, residual, incoming, gate_table, timesteps, positions):
    turned_queries = rotate(queries, positions)
    turned_keys = rotate(keys, positions)
    head_queries, head_keys, head_values = (
        lax.all_to_all(turned_queries, "head", split_axis=2, concat_axis=1, tiled=True),
        lax.all_to_all(turned_keys, "head", split_axis=2, concat_axis=1, tiled=True),
        lax.all_to_all(values, "head", split_axis=2, concat_axis=1, tiled=True),
    )
    frame_index = lax.axis_index("frame")
    last_index = lax.axis_size("frame") - 1
    has_before = frame_index > 0
    has_after = frame_index < last_index
    own_pairs = jnp.stack((head_keys[0], head_values[0]))
    frame_pairs = lax.all_gather(own_pairs, "tok", axis=1, tiled=True)
    prior_pairs = shifted(frame_pairs, "frame", 1)
    later_pairs = shifted(frame_pairs, "frame", -1)
    query_count = head_queries.shape[1]
    score_scale = 1.0 / math.sqrt(HD)
    block_rows = math.gcd(query_count, 512)
    key_blocks = [
        (frame_pairs[0], frame_pairs[1], True),
        (prior_pairs[0], prior_pairs[1], has_before),
        (later_pairs[0], later_pairs[1], has_after),
    ]
    query_blocks = head_queries[0].reshape(query_count // block_rows, block_rows, HD)

    def one_block(query_rows):
        return attend(query_rows, key_blocks, score_scale)

    finished = lax.map(one_block, query_blocks)
    head_outputs = finished.reshape(query_count, HD)
    attention = head_outputs[None]
    returned = lax.all_to_all(attention, "head", split_axis=1, concat_axis=2, tiled=True)
    step_column = jnp.arange(gate_table.shape[0], dtype=jnp.int32)[:, None]
    gate_row = jnp.sum(jnp.where(step_column == timesteps[0], gate_table, 0.0), axis=0)
    updated = (residual.astype(jnp.float32) + gate_row * returned.astype(jnp.float32)).astype(
        jnp.bfloat16
    )
    arriving = shifted(updated, "frame", -1)
    next_queue = jnp.where(frame_index == last_index, incoming[None], arriving)
    departed = from_root(updated, "frame", 0)
    column_count = updated.shape[2] // lax.axis_size("frame")
    leaving = lax.dynamic_slice_in_dim(departed[0], frame_index * column_count, column_count, 1)
    return (next_queue, leaving)


def solution(mesh):
    placed = (
        P("frame", ("head", "tok"), None),
        P("frame", ("head", "tok"), None),
        P("frame", ("head", "tok"), None),
        P("frame", ("head", "tok"), None),
        P(("head", "tok"), None),
        P(),
        P("frame"),
        P("frame"),
    )
    return jax.shard_map(
        per_device,
        mesh=mesh,
        in_specs=placed,
        out_specs=(P("frame", ("head", "tok"), None), P(("head", "tok"), "frame")),
        check_vma=False,
    )
```

profile of v0, /device:TPU:0, one launch (start us, length us, event | category | flops | bytes accessed | tf_op | source)
XLA Modules:
  0.0 130.7 jit_solution(11281220370018225395)
XLA Ops:
  7.2 1.0 copy.54
  8.2 0.9 copy-done.1
  10.3 0.5 broadcast.139
  10.8 1.4 %reduce.2 = bf16[512,96]{1,0:T(8,128)(2,1)S(1)} reduce(bf16[512,1,96]{2,1,0:T(2,128)(2,1)S(1)} %bitcast.97, bf16[]{:T(256)} %broadcast.139), dimensions={1}, to_apply=%bitcast.68.reduce_sub_computation | reduce | bytes 196610
  12.2 0.9 reshape.189
  13.0 6.4 %all-to-all-start.1 = ((bf16[4,2,6144]{2,1,0:T(2,128)(2,1)}), bf16[4,2,6144]{2,1,0:T(2,128)(2,1)S(1)}, u32[]{:S(2)}, u32[]{:S(2)}) async-start(bf16[4,2,6144]{2,1,0:T(2,128)(2,1)} %reshape.189), calls=%async_computation.1 | async-start | bytes 196608 | tf_op jit(solution)/shard_map/all_to_all | solution.py:83
  19.7 1.4 %reduce.1 = bf16[512,96]{1,0:T(8,128)(2,1)S(1)} reduce(bf16[512,1,96]{2,1,0:T(2,128)(2,1)S(1)} %bitcast.102, bf16[]{:T(256)} %broadcast.139), dimensions={1}, to_apply=%bitcast.47.reduce_sub_computation | reduce | bytes 196610
  21.0 0.9 reshape.187
  21.9 3.4 %all-to-all-done.1 = bf16[4,2,6144]{2,1,0:T(2,128)(2,1)S(1)} async-done(((bf16[4,2,6144]{2,1,0:T(2,128)(2,1)}), bf16[4,2,6144]{2,1,0:T(2,128)(2,1)S(1)}, u32[]{:S(2)}, u32[]{:S(2)}) %all-to-all-start.1) | async-done | bytes 98336 | tf_op jit(solution)/shard_map/all_to_all | solution.py:83
  25.3 3.3 %all-to-all-start.2 = ((bf16[4,2,6144]{2,1,0:T(2,128)(2,1)}), bf16[4,2,6144]{2,1,0:T(2,128)(2,1)S(1)}, u32[]{:S(2)}, u32[]{:S(2)}) async-start(bf16[4,2,6144]{2,1,0:T(2,128)(2,1)} %reshape.187), calls=%async_computation.2 | async-start | bytes 196608 | tf_op jit(solution)/shard_map/all_to_all | solution.py:84
  29.0 5.4 %all-to-all-done.2 = bf16[4,2,6144]{2,1,0:T(2,128)(2,1)S(1)} async-done(((bf16[4,2,6144]{2,1,0:T(2,128)(2,1)}), bf16[4,2,6144]{2,1,0:T(2,128)(2,1)S(1)}, u32[]{:S(2)}, u32[]{:S(2)}) %all-to-all-start.2) | async-done | bytes 98336 | tf_op jit(solution)/shard_map/all_to_all | solution.py:84
  34.8 2.1 %all_gather.3 = bf16[2,768,128]{2,1,0:T(8,128)(2,1)S(1)} all-gather(bf16[2,384,128]{2,1,0:T(8,128)(2,1)S(1)} %pad_maximum_fusion), channel_id=1, replica_groups=mesh['frame'=4,'head'=4,'tok'=2] {'tok'}, dimensions={1}, use_global_device_ids=true | all-gather | bytes 589824 | tf_op jit(solution)/shard_map/all_gather | solution.py:91
  36.9 3.4 %collective-permute-start = (bf16[2,768,128]{2,1,0:T(8,128)(2,1)S(1)}, bf16[2,768,128]{2,1,0:T(8,128)(2,1)S(1)}, u32[]{:S(2)}, u32[]{:S(2)}) collective-permute-start(bf16[2,768,128]{2,1,0:T(8,128)(2,1)S(1)} %all_gather.3), channel_id=1, source_target_pairs={{0,8},{8,16},{16,24},{1,9},{9,17},{17,25},{2,10},{10,18},{18,26},{... | collective-permute-start | bytes 1179656 | tf_op jit(solution)/shard_map/ppermute | solution.py:18
  40.6 1.4 %reduce = bf16[512,96]{1,0:T(8,128)(2,1)S(1)} reduce(bf16[512,1,96]{2,1,0:T(2,128)(2,1)S(1)} %bitcast.98, bf16[]{:T(256)} %broadcast.139), dimensions={1}, to_apply=%bitcast.69.reduce_sub_computation | reduce | bytes 196610
  41.9 0.9 reshape.185
  42.8 3.3 %all-to-all-start = ((bf16[4,2,6144]{2,1,0:T(2,128)(2,1)}), bf16[4,2,6144]{2,1,0:T(2,128)(2,1)S(1)}, u32[]{:S(2)}, u32[]{:S(2)}) async-start(bf16[4,2,6144]{2,1,0:T(2,128)(2,1)} %reshape.185), calls=%async_computation | async-start | bytes 196608 | tf_op jit(solution)/shard_map/all_to_all | solution.py:82
  46.8 1.3 collective-permute-start.1
  48.1 3.8 %all-to-all-done = bf16[4,2,6144]{2,1,0:T(2,128)(2,1)S(1)} async-done(((bf16[4,2,6144]{2,1,0:T(2,128)(2,1)}), bf16[4,2,6144]{2,1,0:T(2,128)(2,1)S(1)}, u32[]{:S(2)}, u32[]{:S(2)}) %all-to-all-start) | async-done | bytes 98336 | tf_op jit(solution)/shard_map/all_to_all | solution.py:82
  52.4 7.2 %collective-permute-done.1 = bf16[2,768,128]{2,1,0:T(8,128)(2,1)S(1)} collective-permute-done((bf16[2,768,128]{2,1,0:T(8,128)(2,1)S(1)}, bf16[2,768,128]{2,1,0:T(8,128)(2,1)S(1)}, u32[]{:S(2)}, u32[]{:S(2)}) %collective-permute-start.1) | collective-permute-done | bytes 393248 | tf_op jit(solution)/shard_map/ppermute | solution.py:18
  59.6 7.2 %while.10 = (s32[]{:T(128)}, bf16[3,128,128]{2,1,0:T(8,128)(2,1)S(1)}, bf16[3,128,128]{2,1,0:T(8,128)(2,1)S(1)}, bf16[768,128]{1,0:T(8,128)(2,1)S(1)}, pred[]{:T...) while((s32[]{:T(128)}, ...), condition=%wide.region_8.9_spmd, body=%wide.region_1.8_spmd.sunk | while | flops 153273088 | bytes 5125259 | solution.py:107
  61.7 0.3 fusion.78
  64.1 0.3 fusion.78
  66.9 1.1 reduce.3
  68.1 0.7 reshape.191
  68.7 4.9 %all-to-all-start.3 = ((bf16[4,2,6144]{2,1,0:T(2,128)(2,1)}), bf16[4,2,6144]{2,1,0:T(2,128)(2,1)S(1)}, u32[]{:S(2)}, u32[]{:S(2)}) async-start(bf16[4,2,6144]{2,1,0:T(2,128)(2,1)} %reshape.191), calls=%async_computation.3 | async-start | bytes 196608 | tf_op jit(solution)/shard_map/all_to_all | solution.py:110
  73.8 5.7 %all-to-all-done.3 = bf16[4,2,6144]{2,1,0:T(2,128)(2,1)S(1)} async-done(((bf16[4,2,6144]{2,1,0:T(2,128)(2,1)}), bf16[4,2,6144]{2,1,0:T(2,128)(2,1)S(1)}, u32[]{:S(2)}, u32[]{:S(2)}) %all-to-all-start.3) | async-done | bytes 98336 | tf_op jit(solution)/shard_map/all_to_all | solution.py:110
  79.8 0.7 copy-done.3
  80.5 0.7 broadcast_select_fusion.2
  81.2 1.4 %collective-permute-start.2 = (bf16[1,96,512]{2,1,0:T(8,128)(2,1)S(1)}, bf16[1,96,512]{2,1,0:T(8,128)(2,1)S(1)}, u32[]{:S(2)}, u32[]{:S(2)}) collective-permute-start(bf16[1,96,512]{2,1,0:T(8,128)(2,1)S(1)} %get-tuple-element.89), channel_id=1, source_target_pairs={{8,0},{16,8},{24,16},{9,1},{17,9},{25,17},{10,2},{18,10},{26,18},{... | collective-permute-start | bytes 294920 | tf_op jit(solution)/shard_map/ppermute | solution.py:18
  82.7 39.2 %all-reduce.2.cloned.1.call-done = bf16[1,96,512]{2,1,0:T(8,128)(2,1)} async-done(((bf16[1,96,512]{2,1,0:T(8,128)(2,1)}), bf16[1,96,512]{2,1,0:T(8,128)(2,1)}) %all-reduce.2.cloned.1.call-update) | async-done | bytes 98320 | tf_op jit(solution)/shard_map/psum | solution.py:23
  121.9 1.3 %dynamic-slice_bitcast_fusion = bf16[96,128]{1,0:T(8,128)(2,1)} fusion(bf16[1,96,512]{2,1,0:T(8,128)(2,1)} %all-reduce.2.cloned.1.call-done, s32[]{:T(128)S(6)} %select_n.90), kind=kLoop, calls=%fused_computation.62 | loop fusion | bytes 49156 | tf_op jit(solution)/shard_map/dynamic_slice | solution.py:120
  123.2 0.7 bitcast_select_fusion
  (73 shorter events, 9.0 us)
Async XLA Ops:
  8.2 0.9 copy-start.1
  13.0 6.5 %copy-start.2 = (bf16[1,96,512]{2,1,0:T(8,128)(2,1)S(1)}, bf16[1,96,512]{2,1,0:T(8,128)(2,1)}, u32[]{:S(2)}) copy-start(bf16[1,96,512]{2,1,0:T(8,128)(2,1)} %param.12) | copy-start | bytes 294916
  13.0 12.3 %all-to-all-start.1 = ((bf16[4,2,6144]{2,1,0:T(2,128)(2,1)}), bf16[4,2,6144]{2,1,0:T(2,128)(2,1)S(1)}, u32[]{:S(2)}, u32[]{:S(2)}) async-start(bf16[4,2,6144]{2,1,0:T(2,128)(2,1)} %reshape.189), calls=%async_computation.1 | async-start | bytes 196608 | tf_op jit(solution)/shard_map/all_to_all | solution.py:83
  25.3 9.1 %all-to-all-start.2 = ((bf16[4,2,6144]{2,1,0:T(2,128)(2,1)}), bf16[4,2,6144]{2,1,0:T(2,128)(2,1)S(1)}, u32[]{:S(2)}, u32[]{:S(2)}) async-start(bf16[4,2,6144]{2,1,0:T(2,128)(2,1)} %reshape.187), calls=%async_computation.2 | async-start | bytes 196608 | tf_op jit(solution)/shard_map/all_to_all | solution.py:84
  36.9 15.4 %collective-permute-start = (bf16[2,768,128]{2,1,0:T(8,128)(2,1)S(1)}, bf16[2,768,128]{2,1,0:T(8,128)(2,1)S(1)}, u32[]{:S(2)}, u32[]{:S(2)}) collective-permute-start(bf16[2,768,128]{2,1,0:T(8,128)(2,1)S(1)} %all_gather.3), channel_id=1, source_target_pairs={{0,8},{8,16},{16,24},{1,9},{9,17},{17,25},{2,10},{10,18},{18,26},{... | collective-permute-start | bytes 1179656 | tf_op jit(solution)/shard_map/ppermute | solution.py:18
  42.8 9.1 %all-to-all-start = ((bf16[4,2,6144]{2,1,0:T(2,128)(2,1)}), bf16[4,2,6144]{2,1,0:T(2,128)(2,1)S(1)}, u32[]{:S(2)}, u32[]{:S(2)}) async-start(bf16[4,2,6144]{2,1,0:T(2,128)(2,1)} %reshape.185), calls=%async_computation | async-start | bytes 196608 | tf_op jit(solution)/shard_map/all_to_all | solution.py:82
  46.8 12.8 %collective-permute-start.1 = (bf16[2,768,128]{2,1,0:T(8,128)(2,1)S(1)}, bf16[2,768,128]{2,1,0:T(8,128)(2,1)S(1)}, u32[]{:S(2)}, u32[]{:S(2)}) collective-permute-start(bf16[2,768,128]{2,1,0:T(8,128)(2,1)S(1)} %all_gather.3), channel_id=1, source_target_pairs={{8,0},{16,8},{24,16},{9,1},{17,9},{25,17},{10,2},{18,10},{26,18},{... | collective-permute-start | bytes 1179656 | tf_op jit(solution)/shard_map/ppermute | solution.py:18
  68.7 4.9 %copy-start = (f32[50,512]{1,0:T(8,128)S(1)}, f32[50,512]{1,0:T(8,128)}, u32[]{:S(2)}) copy-start(f32[50,512]{1,0:T(8,128)} %param.15) | copy-start | bytes 307204
  68.7 10.7 %all-to-all-start.3 = ((bf16[4,2,6144]{2,1,0:T(2,128)(2,1)}), bf16[4,2,6144]{2,1,0:T(2,128)(2,1)S(1)}, u32[]{:S(2)}, u32[]{:S(2)}) async-start(bf16[4,2,6144]{2,1,0:T(2,128)(2,1)} %reshape.191), calls=%async_computation.3 | async-start | bytes 196608 | tf_op jit(solution)/shard_map/all_to_all | solution.py:110
  73.6 48.2 %all-reduce.2.cloned.1.call-start = ((), (), s32[]{:S(2)}) async-start(), calls=%async_computation.4 | async-start | bytes 196608 | tf_op jit(solution)/shard_map/psum | solution.py:23
  79.6 0.9 copy-start.3
  81.2 42.0 %copy-start.4 = (bf16[96,512]{1,0:T(8,128)(2,1)S(1)}, bf16[96,512]{1,0:T(8,128)(2,1)}, u32[]{:S(2)}) copy-start(bf16[96,512]{1,0:T(8,128)(2,1)} %param.14) | copy-start | bytes 294916
  81.2 42.0 %collective-permute-start.2 = (bf16[1,96,512]{2,1,0:T(8,128)(2,1)S(1)}, bf16[1,96,512]{2,1,0:T(8,128)(2,1)S(1)}, u32[]{:S(2)}, u32[]{:S(2)}) collective-permute-start(bf16[1,96,512]{2,1,0:T(8,128)(2,1)S(1)} %get-tuple-element.89), channel_id=1, source_target_pairs={{8,0},{16,8},{24,16},{9,1},{17,9},{25,17},{10,2},{18,10},{26,18},{... | collective-permute-start | bytes 294920 | tf_op jit(solution)/shard_map/ppermute | solution.py:18
Sparse Core Ops, SparseCore 0:
  81.3 40.5 all-reduce.1
where the time goes:
time: 132 us; the launch traced here: 131 us
  waiting for transfers between devices  64.8 us (49%)
  starting transfers between devices  24.1 us (18%)
  between operations  15.7 us (12%)
  local copies, waits for them, and re-layouts  10 us (8%)
  other arithmetic  8.48 us (6%)
  matrix products  5.4 us (4%)
  blocking collectives  2.09 us (2%)
    psum x1, waiting for transfers between devices, from_root(): return lax.psum(block, axis)  39.2 us
    unnamed x22, local copies, waits for them, and re-layouts  7.35 us
    ppermute x3, waiting for transfers between devices, shifted(): return lax.ppermute(block, axis, route)  7.2 us
    all_to_all x1, starting transfers between devices, per_device(): lax.all_to_all(turned_keys, 'head', split_axis=2, concat_axis=1, tiled=True)  6.45 us
    ppermute x3, starting transfers between devices, shifted(): return lax.ppermute(block, axis, route)  6.12 us
    all_to_all x1, waiting for transfers between devices, per_device(): lax.all_to_all(attention, 'head', split_axis=1, concat_axis=2, tiled=True)  5.71 us
    all_to_all x1, waiting for transfers between devices, per_device(): lax.all_to_all(values, 'head', split_axis=2, concat_axis=1, tiled=True)  5.41 us
    unnamed x4, other arithmetic  5.19 us
  transfers between devices with their start and end apart: 8, of which 6 were waited for; matrix products, arithmetic and copies ran while one was open for 5% of the time, Pallas kernels for 0%

commit v1 on v0

v1 whole, which is shorter than its diff:
```python
import functools
import math

import jax
import jax.numpy as jnp
from jax import lax
from jax.experimental import pallas as pl
from jax.experimental.pallas import tpu as pltpu
from jax.sharding import PartitionSpec as P

HD = 128
HALF = 8
MESH = pl.DeviceIdType.MESH
ABSENT = 1e30


def kernel(
    frames, heads, relay,
    q_hbm, k_hbm, v_hbm, res_hbm, inc_hbm, gate_hbm, steps_ref, pos_ref,
    nq_ref, lv_ref,
    q_in, k_in, gate_in, kv_out, q_out, gate_out,
    kv_buf, q_buf, o_out, o_buf, lo_buf, res_buf, lres_buf, gate_buf, lgate_buf, nq_buf, lv_buf,
    load_sem, v_sem, kvz_s, kvz_r, qz_s, qz_r, peer_s, peer_r, fr_s, fr_r, rl_s, fwd_s, fwd_r,
    o_s, o_r, lo_r, res_s, res_r, lres_s, lres_r, gate_s, gate_r, lgate_s, lgate_r, out_sem,
):
    F, Z = frames, heads
    f = lax.axis_index("frame")
    h = lax.axis_index("head")
    t = lax.axis_index("tok")
    T = q_in.shape[0]
    has_prev = f > 0
    has_next = f < F - 1

    def at(fr, hd, tk):
        return {"frame": fr, "head": hd, "tok": tk}

    def remote(src, dst, send, recv, dev):
        return pltpu.make_async_remote_copy(
            src_ref=src, dst_ref=dst, send_sem=send, recv_sem=recv, device_id=dev, device_id_type=MESH
        )

    load_k = pltpu.make_async_copy(k_hbm.at[0], k_in, load_sem.at[0])
    load_q = pltpu.make_async_copy(q_hbm.at[0], q_in, load_sem.at[1])
    load_gate = pltpu.make_async_copy(gate_hbm, gate_in, load_sem.at[2])
    load_v = [
        pltpu.make_async_copy(v_hbm.at[0, :, pl.ds(j * HD, HD)], kv_out.at[j, 1], v_sem.at[j]) for j in range(Z)
    ]
    load_k.start()
    for c in load_v:
        c.start()
    load_q.start()
    load_gate.start()

    barrier = pltpu.get_barrier_semaphore()
    me = f * Z + h

    def greet(s, carry):
        other = lax.rem(me + s, F * Z)
        pl.semaphore_signal(barrier, inc=1, device_id=at(other // Z, lax.rem(other, Z), t), device_id_type=MESH)
        return carry

    lax.fori_loop(1, F * Z, greet, 0)
    pl.semaphore_signal(barrier, inc=1, device_id=at(f, h, 1 - t), device_id_type=MESH)

    lane = lax.broadcasted_iota(jnp.int32, (8, HD), 1)
    power = lax.rem(lane, HALF).astype(jnp.float32)
    angle = pos_ref[0].astype(jnp.float32) * jnp.exp2(-power)
    cosine = jnp.where(lane < 2 * HALF, jnp.cos(angle), 1.0)[0:1]
    sine = jnp.sin(angle)
    sine_up = jnp.where(lane < HALF, -sine, 0.0)[0:1]
    sine_down = jnp.where((lane >= HALF) & (lane < 2 * HALF), sine, 0.0)[0:1]

    def turned(x):
        x = x.astype(jnp.float32)
        up = pltpu.roll(x, HD - HALF, 1)
        down = pltpu.roll(x, HALF, 1)
        return (x * cosine + up * sine_up + down * sine_down).astype(jnp.bfloat16)

    load_k.wait()
    for j in range(Z):
        kv_out[j, 0] = turned(k_in[:, j * HD : (j + 1) * HD])
    load_q.wait()
    for j in range(Z):
        q_out[j] = turned(q_in[:, j * HD : (j + 1) * HD])
    for c in load_v:
        c.wait()
    pl.semaphore_wait(barrier, F * Z)

    def kv_send(s):
        d = lax.rem(h + s, Z)
        return remote(kv_out.at[d], kv_buf.at[0, t, h], kvz_s.at[s], kvz_r.at[s], at(f, d, t))

    def q_send(s):
        d = lax.rem(h + s, Z)
        return remote(q_out.at[d], q_buf.at[h], qz_s.at[s], qz_r.at[s], at(f, d, t))

    for s in range(1, Z):
        kv_send(s).start()

    def peer_send(s, b, src):
        return remote(src, kv_buf.at[0, t, b], peer_s.at[s], peer_r.at[s], at(f, h, 1 - t))

    def next_send(s, b, src):
        return remote(src, kv_buf.at[1, t, b], fr_s.at[0, s], fr_r.at[0, s], at(f + 1, h, t))

    def prev_send(s, b, src):
        return remote(src, kv_buf.at[2, t, b], fr_s.at[1, s], fr_r.at[1, s], at(f - 1, h, t))

    sends_next = has_next
    sends_prev = has_prev
    if relay:
        sends_next = has_next & (f != 1)
        sends_prev = has_prev & (f != 2)

    def spread(s, b, src):
        @pl.when(sends_next)
        def _():
            next_send(s, b, src).start()

        @pl.when(sends_prev)
        def _():
            prev_send(s, b, src).start()

        peer_send(s, b, src).start()

    spread(0, h, kv_out.at[h])
    for s in range(1, Z):
        q_send(s).start()
    kv_buf[0, t, h] = kv_out[h]
    q_buf[h] = q_out[h]

    load_gate.wait()
    gate_out[...] = jnp.broadcast_to(gate_in[pl.ds(steps_ref[0], 1), :], gate_out.shape)

    def res_send():
        return remote(res_hbm, res_buf, res_s, res_r, at(f - 1, h, t))

    def gate_send():
        return remote(gate_out, gate_buf, gate_s, gate_r, at(f - 1, h, t))

    def lres_send(g):
        return remote(res_hbm.at[0, :, pl.ds(g * HD, HD)], lres_buf, lres_s.at[g], lres_r, at(g, h, t))

    def lgate_send(g):
        return remote(gate_out.at[:, pl.ds(g * HD, HD)], lgate_buf, lgate_s.at[g], lgate_r, at(g, h, t))

    @pl.when(has_prev)
    def _():
        res_send().start()
        gate_send().start()

    @pl.when(f == 0)
    def _():
        pltpu.make_async_copy(res_hbm.at[0, :, pl.ds(0, HD)], lres_buf, lres_r).start()
        pltpu.make_async_copy(gate_out.at[:, pl.ds(0, HD)], lgate_buf, lgate_r).start()
        for g in range(1, F):
            lres_send(g).start()
            lgate_send(g).start()
        kv_buf[1] = jnp.zeros(kv_buf.shape[1:], kv_buf.dtype)

    @pl.when(f == F - 1)
    def _():
        kv_buf[2] = jnp.zeros(kv_buf.shape[1:], kv_buf.dtype)

    for s in range(1, Z):
        b = lax.rem(h + Z - s, Z)
        remote(kv_out.at[0], kv_buf.at[0, t, b], kvz_s.at[s], kvz_r.at[s], at(f, b, t)).wait_recv()
        spread(s, b, kv_buf.at[0, t, b])

    def fwd_send(slot, s, b):
        ref = kv_buf.at[slot, t, b]
        return remote(ref, ref, fwd_s.at[slot - 1, s], fwd_r.at[slot - 1, s], at(f, h, 1 - t))

    def relay_down(s, b):
        return remote(kv_buf.at[2, t, b], kv_buf.at[1, t, b], rl_s.at[s], fr_r.at[0, s], at(2, h, t))

    def relay_up(s, b):
        return remote(kv_buf.at[1, t, b], kv_buf.at[2, t, b], rl_s.at[s], fr_r.at[1, s], at(1, h, t))

    for s in range(Z):
        b = lax.rem(h + Z - s, Z)

        @pl.when(has_prev)
        def _():
            remote(kv_out.at[0], kv_buf.at[1, t, b], fr_s.at[0, s], fr_r.at[0, s], at(f, h, 1 - t)).wait_recv()
            if relay:

                @pl.when(f == 3)
                def _():
                    relay_up(s, b).start()

            fwd_send(1, s, b).start()

        @pl.when(has_next)
        def _():
            remote(kv_out.at[0], kv_buf.at[2, t, b], fr_s.at[1, s], fr_r.at[1, s], at(f, h, 1 - t)).wait_recv()
            if relay:

                @pl.when(f == 0)
                def _():
                    relay_down(s, b).start()

            fwd_send(2, s, b).start()

    for s in range(Z):
        b = lax.rem(h + Z - s, Z)
        remote(kv_out.at[0], kv_buf.at[0, 1 - t, b], peer_s.at[s], peer_r.at[s], at(f, h, 1 - t)).wait_recv()
        if s > 0:
            remote(q_out.at[0], q_buf.at[b], qz_s.at[s], qz_r.at[s], at(f, b, t)).wait_recv()

        @pl.when(has_prev)
        def _():
            remote(
                kv_out.at[0], kv_buf.at[1, 1 - t, b], fwd_s.at[0, s], fwd_r.at[0, s], at(f, h, 1 - t)
            ).wait_recv()

        @pl.when(has_next)
        def _():
            remote(
                kv_out.at[0], kv_buf.at[2, 1 - t, b], fwd_s.at[1, s], fwd_r.at[1, s], at(f, h, 1 - t)
            ).wait_recv()

    group = 2 if Z <= 4 else 1
    masks = (
        jnp.float32(0.0),
        jnp.where(has_prev, 0.0, ABSENT).astype(jnp.float32),
        jnp.where(has_next, 0.0, ABSENT).astype(jnp.float32),
    )
    rate = math.log2(math.e) / math.sqrt(HD)
    keys_all = 2 * Z * T

    def o_send(j):
        return remote(o_out.at[j], o_buf.at[h], o_s.at[j], o_r.at[h], at(f - 1, j, t))

    def lo_send(j):
        return remote(o_out.at[j], lo_buf, o_s.at[j], lo_r, at(h, j, t))

    def attend(i, carry):
        rows = q_buf[pl.ds(i * group, group)].reshape(group * T, HD)
        scores = [
            lax.dot_general(
                rows,
                kv_buf[slot, :, :, 0].reshape(keys_all, HD),
                (((1,), (1,)), ((), ())),
                preferred_element_type=jnp.float32,
            )
            for slot in range(3)
        ]
        highest = jnp.max(scores[0], axis=1, keepdims=True)
        for slot in (1, 2):
            highest = jnp.maximum(highest, jnp.max(scores[slot], axis=1, keepdims=True) - masks[slot])
        total = jnp.zeros((group * T, 1), jnp.float32)
        blended = jnp.zeros((group * T, HD), jnp.float32)
        for slot in range(3):
            weights = jnp.exp2((scores[slot] - (highest + masks[slot])) * rate)
            total = total + jnp.sum(weights, axis=1, keepdims=True)
            blended = blended + jnp.dot(
                weights.astype(jnp.bfloat16),
                kv_buf[slot, :, :, 1].reshape(keys_all, HD),
                preferred_element_type=jnp.float32,
            )
        result = (blended / total).astype(jnp.bfloat16)
        for g in range(group):
            o_out[i * group + g] = result[g * T : (g + 1) * T]
            j = i * group + g

            @pl.when(f > 0)
            def _():
                o_send(j).start()

            @pl.when((f == 0) & ((h != 0) | (j != 0)))
            def _():
                lo_send(j).start()

            @pl.when((f == 0) & (h == 0) & (j == 0))
            def _():
                pltpu.make_async_copy(o_out.at[0], lo_buf, lo_r).start()

        return carry

    lax.fori_loop(0, Z // group, attend, 0)

    @pl.when(f == F - 1)
    def _():
        pltpu.make_async_copy(inc_hbm, nq_ref.at[0], out_sem.at[0]).start()

    @pl.when(f < F - 1)
    def _():
        remote(res_hbm, res_buf, res_s, res_r, at(f, h, 1 - t)).wait_recv()
        remote(gate_out, gate_buf, gate_s, gate_r, at(f, h, 1 - t)).wait_recv()
        for j in range(Z):
            remote(o_out.at[0], o_buf.at[j], o_s.at[0], o_r.at[j], at(f, h, 1 - t)).wait_recv()
            cols = slice(j * HD, (j + 1) * HD)
            nq_buf[:, cols] = (
                res_buf[0, :, cols].astype(jnp.float32) + gate_buf[0:1, cols] * o_buf[j].astype(jnp.float32)
            ).astype(jnp.bfloat16)
        pltpu.make_async_copy(nq_buf, nq_ref.at[0], out_sem.at[0]).start()

    remote(lres_buf, lres_buf, lres_s.at[0], lres_r, at(f, h, 1 - t)).wait_recv()
    remote(lgate_buf, lgate_buf, lgate_s.at[0], lgate_r, at(f, h, 1 - t)).wait_recv()
    remote(lo_buf, lo_buf, o_s.at[0], lo_r, at(f, h, 1 - t)).wait_recv()
    lv_buf[...] = (
        lres_buf[...].astype(jnp.float32) + lgate_buf[0:1, :] * lo_buf[...].astype(jnp.float32)
    ).astype(jnp.bfloat16)
    leave = pltpu.make_async_copy(lv_buf, lv_ref, out_sem.at[1])
    leave.start()

    for s in range(Z):
        if s > 0:
            kv_send(s).wait_send()
            q_send(s).wait_send()
        peer_send(s, 0, kv_out.at[0]).wait_send()

        @pl.when(sends_next)
        def _():
            next_send(s, 0, kv_out.at[0]).wait_send()

        @pl.when(sends_prev)
        def _():
            prev_send(s, 0, kv_out.at[0]).wait_send()

        @pl.when(has_prev)
        def _():
            fwd_send(1, s, 0).wait_send()

        @pl.when(has_next)
        def _():
            fwd_send(2, s, 0).wait_send()

        if relay:

            @pl.when((f == 0) | (f == 3))
            def _():
                relay_down(s, 0).wait_send()

        @pl.when((f > 0) | (h != 0) | (s != 0))
        def _():
            o_send(s).wait_send()

    @pl.when(has_prev)
    def _():
        res_send().wait_send()
        gate_send().wait_send()

    @pl.when(f == 0)
    def _():
        for g in range(1, F):
            lres_send(g).wait_send()
            lgate_send(g).wait_send()

    pltpu.make_async_copy(inc_hbm, nq_ref.at[0], out_sem.at[0]).wait()
    leave.wait()


def solution(mesh):
    F, Z = mesh.shape["frame"], mesh.shape["head"]

    def per_device(queries, keys, values, residual, incoming, gate_table, timesteps, positions):
        T, HH = queries.shape[1], queries.shape[2]
        assert HH == Z * HD and HH == F * HD and mesh.shape["tok"] == 2
        bf, f32 = jnp.bfloat16, jnp.float32
        dma = pltpu.SemaphoreType.DMA
        anywhere = pl.BlockSpec(memory_space=pl.ANY)
        smem = pl.BlockSpec(memory_space=pltpu.SMEM)
        return pl.pallas_call(
            functools.partial(kernel, F, Z, F == 4),
            out_shape=(
                jax.ShapeDtypeStruct((1, T, HH), bf),
                jax.ShapeDtypeStruct((T, HD), bf),
            ),
            in_specs=[anywhere] * 6 + [smem, smem],
            out_specs=(anywhere, anywhere),
            scratch_shapes=[
                pltpu.VMEM((T, HH), bf),
                pltpu.VMEM((T, HH), bf),
                pltpu.VMEM(gate_table.shape, f32),
                pltpu.VMEM((Z, 2, T, HD), bf),
                pltpu.VMEM((Z, T, HD), bf),
                pltpu.VMEM((8, HH), f32),
                pltpu.VMEM((3, 2, Z, 2, T, HD), bf),
                pltpu.VMEM((Z, T, HD), bf),
                pltpu.VMEM((Z, T, HD), bf),
                pltpu.VMEM((Z, T, HD), bf),
                pltpu.VMEM((T, HD), bf),
                pltpu.VMEM((1, T, HH), bf),
                pltpu.VMEM((T, HD), bf),
                pltpu.VMEM((8, HH), f32),
                pltpu.VMEM((8, HD), f32),
                pltpu.VMEM((T, HH), bf),
                pltpu.VMEM((T, HD), bf),
                dma((3,)), dma((Z,)),
                dma((Z,)), dma((Z,)), dma((Z,)), dma((Z,)),
                dma((Z,)), dma((Z,)), dma((2, Z)), dma((2, Z)), dma((Z,)), dma((2, Z)), dma((2, Z)),
                dma((Z,)), dma((Z,)), dma,
                dma, dma, dma((F,)), dma,
                dma, dma, dma((F,)), dma,
                dma((2,)),
            ],
            compiler_params=pltpu.CompilerParams(
                collective_id=0, has_side_effects=True, vmem_limit_bytes=48 * 1024 * 1024
            ),
        )(queries, keys, values, residual, incoming, gate_table, timesteps, positions)

    placed = (
        P("frame", ("head", "tok"), None),
        P("frame", ("head", "tok"), None),
        P("frame", ("head", "tok"), None),
        P("frame", ("head", "tok"), None),
        P(("head", "tok"), None),
        P(),
        P("frame"),
        P("frame"),
    )
    return jax.shard_map(
        per_device,
        mesh=mesh,
        in_specs=placed,
        out_specs=(P("frame", ("head", "tok"), None), P(("head", "tok"), "frame")),
        check_vma=False,
    )
```

time: 132 us -> 36.1 us (0.27)
  waiting for transfers between devices: 64.8 us -> 0 us
  Pallas kernels: 0 us -> 27.2 us
  starting transfers between devices: 24.1 us -> 0 us
  between operations: 15.7 us -> 1.95 us
  other arithmetic: 8.48 us -> 0 us
  matrix products: 5.4 us -> 0 us
  local copies, waits for them, and re-layouts: 10 us -> 6.6 us
  blocking collectives: 2.09 us -> 0 us
    psum x1 -> x0, waiting for transfers between devices: 39.2 us -> none  [from_root(): return lax.psum(block, axis)]
    pallas_call x0 -> x1, Pallas kernels: none -> 27.2 us  [per_device(): pl.pallas_call(functools.partial(kernel, F, Z, F == 4), out_shape=(jax.Sh...]
    all_to_all x4 -> x0, waiting for transfers between devices: 18.4 us -> none  [the longest x1 5.71 us: per_device(): lax.all_to_all(attention, 'head', split_axis=1, concat_axis=2, tiled=True)]
    all_to_all x4 -> x0, starting transfers between devices: 18 us -> none  [the longest x1 6.45 us: per_device(): lax.all_to_all(turned_keys, 'head', split_axis=2, concat_axis=1, tiled=True)]
    ppermute x3 -> x0, waiting for transfers between devices: 7.2 us -> none  [shifted(): return lax.ppermute(block, axis, route)]
    ppermute x3 -> x0, starting transfers between devices: 6.12 us -> none  [shifted(): return lax.ppermute(block, axis, route)]
    dot_general x18 -> x0, matrix products: 5.4 us -> none  [the longest x9 2.73 us: block_stats(): jnp.einsum('qd,kd->qk', query_rows, block_keys, preferred_element_type=jn...]
    unnamed x4 -> x0, other arithmetic: 5.19 us -> none
  transfers between devices with their start and end apart: 8 -> 0, of which waited for: 6 -> 0; matrix products, arithmetic and copies ran while one was open for 5% -> 0% of each run, Pallas kernels for 0% -> 0%
where the time goes in v1:
time: 36.1 us; the launch traced here: 35.8 us
  Pallas kernels  27.2 us (75%)
  local copies, waits for them, and re-layouts  6.6 us (18%)
  between operations  1.95 us (5%)
    pallas_call x1, Pallas kernels, per_device(): pl.pallas_call(functools.partial(kernel, F, Z, F == 4), out_shape=(jax.Sh...  27.2 us
    unnamed x14, local copies, waits for them, and re-layouts  6.6 us

profile of v1, /device:TPU:0, one launch (start us, length us, event | category | flops | bytes accessed | tf_op | source)
XLA Modules:
  0.0 35.8 jit_solution(621640933041480564)
XLA Ops:
  1.9 0.0 copy-start
  1.9 0.9 %copy-done = f32[50,512]{1,0:T(8,128)S(1)} copy-done((f32[50,512]{1,0:T(8,128)S(1)}, f32[50,512]{1,0:T(8,128)}, u32[]{:S(2)}) %copy-start) | copy-done | bytes 102424
  2.8 0.0 copy-start.1
  2.8 0.9 %copy-done.1 = bf16[1,96,512]{2,1,0:T(8,128)(2,1)S(1)} copy-done((bf16[1,96,512]{2,1,0:T(8,128)(2,1)S(1)}, bf16[1,96,512]{2,1,0:T(8,128)(2,1)}, u32[]{:S(2)}) %copy-start.1) | copy-done | bytes 98328
  3.7 0.0 copy-start.2
  3.7 0.9 %copy-done.2 = bf16[1,96,512]{2,1,0:T(8,128)(2,1)S(1)} copy-done((bf16[1,96,512]{2,1,0:T(8,128)(2,1)S(1)}, bf16[1,96,512]{2,1,0:T(8,128)(2,1)}, u32[]{:S(2)}) %copy-start.2) | copy-done | bytes 98328
  4.6 0.0 copy-start.3
  4.6 0.9 %copy-done.3 = bf16[1,96,512]{2,1,0:T(8,128)(2,1)S(1)} copy-done((bf16[1,96,512]{2,1,0:T(8,128)(2,1)S(1)}, bf16[1,96,512]{2,1,0:T(8,128)(2,1)}, u32[]{:S(2)}) %copy-start.3) | copy-done | bytes 98328
  5.5 0.0 copy-start.4
  5.5 0.9 %copy-done.4 = bf16[1,96,512]{2,1,0:T(8,128)(2,1)S(1)} copy-done((bf16[1,96,512]{2,1,0:T(8,128)(2,1)S(1)}, bf16[1,96,512]{2,1,0:T(8,128)(2,1)}, u32[]{:S(2)}) %copy-start.4) | copy-done | bytes 98328
  6.4 0.0 copy-start.5
  6.4 0.9 %copy-done.5 = bf16[96,512]{1,0:T(8,128)(2,1)S(1)} copy-done((bf16[96,512]{1,0:T(8,128)(2,1)S(1)}, bf16[96,512]{1,0:T(8,128)(2,1)}, u32[]{:S(2)}) %copy-start.5) | copy-done | bytes 98328
  7.3 27.2 %shard_map.95 = (bf16[1,96,512]{2,1,0:T(8,128)(2,1)S(1)}, bf16[96,128]{1,0:T(8,128)(2,1)S(1)}) custom-call(bf16[1,96,512]{2,1,0:T(8,128)(2,1)S(1)} %copy-done.1, bf16[1,96,512]{2,1,0:T(8,128)(2,1)S(1)} %copy-done.2, bf16[1,96,512]{2,1,0:T(8,128)(2,1)S(1)} %copy-done.3, bf16[1,96,512]{2,1,0:T(8,128)(2,1)S(1)} %copy-done.4, bf16[96,512]{1,0:T(8,128)(2,1)S(1)} %copy-done.5, ...), custom_call_target="tpu_custom_call" | custom-call | tf_op jit(solution)/shard_map/pallas_call | solution.py:365
  34.5 0.6 %copy.14 = bf16[1,96,512]{2,1,0:T(8,128)(2,1)} copy(bf16[1,96,512]{2,1,0:T(8,128)(2,1)S(1)} %get-tuple-element.4) | data formatting | bytes 196608
  35.2 0.6 %copy.15 = bf16[96,128]{1,0:T(8,128)(2,1)} copy(bf16[96,128]{1,0:T(8,128)(2,1)S(1)} %get-tuple-element.5) | data formatting | bytes 49152
Async XLA Ops:
  1.9 0.9 %copy-start = (f32[50,512]{1,0:T(8,128)S(1)}, f32[50,512]{1,0:T(8,128)}, u32[]{:S(2)}) copy-start(f32[50,512]{1,0:T(8,128)} %gate_hbm.1) | copy-start | bytes 307204
  2.8 0.9 %copy-start.1 = (bf16[1,96,512]{2,1,0:T(8,128)(2,1)S(1)}, bf16[1,96,512]{2,1,0:T(8,128)(2,1)}, u32[]{:S(2)}) copy-start(bf16[1,96,512]{2,1,0:T(8,128)(2,1)} %q_hbm.1) | copy-start | bytes 294916
  3.7 0.9 %copy-start.2 = (bf16[1,96,512]{2,1,0:T(8,128)(2,1)S(1)}, bf16[1,96,512]{2,1,0:T(8,128)(2,1)}, u32[]{:S(2)}) copy-start(bf16[1,96,512]{2,1,0:T(8,128)(2,1)} %k_hbm.1) | copy-start | bytes 294916
  4.6 0.9 %copy-start.3 = (bf16[1,96,512]{2,1,0:T(8,128)(2,1)S(1)}, bf16[1,96,512]{2,1,0:T(8,128)(2,1)}, u32[]{:S(2)}) copy-start(bf16[1,96,512]{2,1,0:T(8,128)(2,1)} %v_hbm.1) | copy-start | bytes 294916
  5.5 0.9 %copy-start.4 = (bf16[1,96,512]{2,1,0:T(8,128)(2,1)S(1)}, bf16[1,96,512]{2,1,0:T(8,128)(2,1)}, u32[]{:S(2)}) copy-start(bf16[1,96,512]{2,1,0:T(8,128)(2,1)} %res_hbm.1) | copy-start | bytes 294916
  6.4 0.9 %copy-start.5 = (bf16[96,512]{1,0:T(8,128)(2,1)S(1)}, bf16[96,512]{1,0:T(8,128)(2,1)}, u32[]{:S(2)}) copy-start(bf16[96,512]{1,0:T(8,128)(2,1)} %inc_hbm.1) | copy-start | bytes 294916

commit v2 on v1

--- a/solution.py
+++ b/solution.py
@@ -11,7 +11,6 @@
 HD = 128
 HALF = 8
 MESH = pl.DeviceIdType.MESH
-ABSENT = 1e30
 
 
 def kernel(
@@ -20,7 +19,8 @@
     nq_ref, lv_ref,
     q_in, k_in, gate_in, kv_out, q_out, gate_out,
     kv_buf, q_buf, o_out, o_buf, lo_buf, res_buf, lres_buf, gate_buf, lgate_buf, nq_buf, lv_buf,
-    load_sem, v_sem, kvz_s, kvz_r, qz_s, qz_r, peer_s, peer_r, fr_s, fr_r, rl_s, fwd_s, fwd_r,
+    top, weight_sum, blended_buf,
+    load_sem, v_sem, kvz_s, kvz_r, qz_s, qz_r, peer_s, peer_r, fr_s, fr_r, fwd_s, fwd_r,
     o_s, o_r, lo_r, res_s, res_r, lres_s, lres_r, gate_s, gate_r, lgate_s, lgate_r, out_sem,
 ):
     F, Z = frames, heads
@@ -29,7 +29,9 @@
     t = lax.axis_index("tok")
     T = q_in.shape[0]
     has_prev = f > 0
-    has_next = f < F - 1
+    has_across = (f > 0) & (f < F - 1)
+    partner = f + 1 - 2 * lax.rem(f, 2)
+    across = f - 1 + 2 * lax.rem(f, 2)
 
     def at(fr, hd, tk):
         return {"frame": fr, "head": hd, "tok": tk}
@@ -92,7 +94,7 @@
 
     def q_send(s):
         d = lax.rem(h + s, Z)
-        return remote(q_out.at[d], q_buf.at[h], qz_s.at[s], qz_r.at[s], at(f, d, t))
+        return remote(q_out.at[d], q_buf.at[s], qz_s.at[s], qz_r.at[s], at(f, d, t))
 
     for s in range(1, Z):
         kv_send(s).start()
@@ -100,26 +102,28 @@
     def peer_send(s, b, src):
         return remote(src, kv_buf.at[0, t, b], peer_s.at[s], peer_r.at[s], at(f, h, 1 - t))
 
-    def next_send(s, b, src):
-        return remote(src, kv_buf.at[1, t, b], fr_s.at[0, s], fr_r.at[0, s], at(f + 1, h, t))
-
-    def prev_send(s, b, src):
-        return remote(src, kv_buf.at[2, t, b], fr_s.at[1, s], fr_r.at[1, s], at(f - 1, h, t))
-
-    sends_next = has_next
-    sends_prev = has_prev
-    if relay:
-        sends_next = has_next & (f != 1)
-        sends_prev = has_prev & (f != 2)
+    def pair_send(s, b, src):
+        return remote(src, kv_buf.at[1, t, b], fr_s.at[0, s], fr_r.at[0, s], at(partner, h, t))
+
+    def across_send(s, b, src):
+        return remote(src, kv_buf.at[2, t, b], fr_s.at[1, s], fr_r.at[1, s], at(across, h, t))
+
+    def relay_send(s, b):
+        return remote(
+            kv_buf.at[1, t, b], kv_buf.at[2, t, b], fr_s.at[1, s], fr_r.at[1, s], at(lax.rem(f + 2, F), h, t)
+        )
+
+    def fwd_send(slot, s, b):
+        ref = kv_buf.at[slot, t, b]
+        return remote(ref, ref, fwd_s.at[slot - 1, s], fwd_r.at[slot - 1, s], at(f, h, 1 - t))
 
     def spread(s, b, src):
-        @pl.when(sends_next)
-        def _():
-            next_send(s, b, src).start()
-
-        @pl.when(sends_prev)
-        def _():
-            prev_send(s, b, src).start()
+        pair_send(s, b, src).start()
+        if not relay:
+
+            @pl.when(has_across)
+            def _():
+                across_send(s, b, src).start()
 
         peer_send(s, b, src).start()
 
@@ -127,10 +131,29 @@
     for s in range(1, Z):
         q_send(s).start()
     kv_buf[0, t, h] = kv_out[h]
-    q_buf[h] = q_out[h]
+    q_buf[0] = q_out[h]
 
     load_gate.wait()
     gate_out[...] = jnp.broadcast_to(gate_in[pl.ds(steps_ref[0], 1), :], gate_out.shape)
+
+    def came(ref, sem):
+        remote(ref, ref, sem, sem, at(f, h, 1 - t)).wait_recv()
+
+    for s in range(1, Z):
+        b = lax.rem(h + Z - s, Z)
+        came(kv_buf.at[0, t, b], kvz_r.at[s])
+        spread(s, b, kv_buf.at[0, t, b])
+
+    for s in range(Z):
+        b = lax.rem(h + Z - s, Z)
+        came(kv_buf.at[1, t, b], fr_r.at[0, s])
+        if relay:
+
+            @pl.when(jnp.logical_not(has_across))
+            def _():
+                relay_send(s, b).start()
+
+        fwd_send(1, s, b).start()
 
     def res_send():
         return remote(res_hbm, res_buf, res_s, res_r, at(f - 1, h, t))
@@ -156,129 +179,115 @@
         for g in range(1, F):
             lres_send(g).start()
             lgate_send(g).start()
-        kv_buf[1] = jnp.zeros(kv_buf.shape[1:], kv_buf.dtype)
-
-    @pl.when(f == F - 1)
-    def _():
-        kv_buf[2] = jnp.zeros(kv_buf.shape[1:], kv_buf.dtype)
-
-    for s in range(1, Z):
-        b = lax.rem(h + Z - s, Z)
-        remote(kv_out.at[0], kv_buf.at[0, t, b], kvz_s.at[s], kvz_r.at[s], at(f, b, t)).wait_recv()
-        spread(s, b, kv_buf.at[0, t, b])
-
-    def fwd_send(slot, s, b):
-        ref = kv_buf.at[slot, t, b]
-        return remote(ref, ref, fwd_s.at[slot - 1, s], fwd_r.at[slot - 1, s], at(f, h, 1 - t))
-
-    def relay_down(s, b):
-        return remote(kv_buf.at[2, t, b], kv_buf.at[1, t, b], rl_s.at[s], fr_r.at[0, s], at(2, h, t))
-
-    def relay_up(s, b):
-        return remote(kv_buf.at[1, t, b], kv_buf.at[2, t, b], rl_s.at[s], fr_r.at[1, s], at(1, h, t))
 
     for s in range(Z):
-        b = lax.rem(h + Z - s, Z)
-
-        @pl.when(has_prev)
-        def _():
-            remote(kv_out.at[0], kv_buf.at[1, t, b], fr_s.at[0, s], fr_r.at[0, s], at(f, h, 1 - t)).wait_recv()
-            if relay:
-
-                @pl.when(f == 3)
-                def _():
-                    relay_up(s, b).start()
-
-            fwd_send(1, s, b).start()
-
-        @pl.when(has_next)
-        def _():
-            remote(kv_out.at[0], kv_buf.at[2, t, b], fr_s.at[1, s], fr_r.at[1, s], at(f, h, 1 - t)).wait_recv()
-            if relay:
-
-                @pl.when(f == 0)
-                def _():
-                    relay_down(s, b).start()
-
-            fwd_send(2, s, b).start()
-
-    for s in range(Z):
-        b = lax.rem(h + Z - s, Z)
-        remote(kv_out.at[0], kv_buf.at[0, 1 - t, b], peer_s.at[s], peer_r.at[s], at(f, h, 1 - t)).wait_recv()
-        if s > 0:
-            remote(q_out.at[0], q_buf.at[b], qz_s.at[s], qz_r.at[s], at(f, b, t)).wait_recv()
-
-        @pl.when(has_prev)
-        def _():
-            remote(
-                kv_out.at[0], kv_buf.at[1, 1 - t, b], fwd_s.at[0, s], fwd_r.at[0, s], at(f, h, 1 - t)
-            ).wait_recv()
-
-        @pl.when(has_next)
-        def _():
-            remote(
-                kv_out.at[0], kv_buf.at[2, 1 - t, b], fwd_s.at[1, s], fwd_r.at[1, s], at(f, h, 1 - t)
-            ).wait_recv()
-
-    group = 2 if Z <= 4 else 1
-    masks = (
-        jnp.float32(0.0),
-        jnp.where(has_prev, 0.0, ABSENT).astype(jnp.float32),
-        jnp.where(has_next, 0.0, ABSENT).astype(jnp.float32),
-    )
+        b = lax.rem(h + s, Z)
+        came(kv_buf.at[0, 1 - t, b], peer_r.at[s])
+
     rate = math.log2(math.e) / math.sqrt(HD)
     keys_all = 2 * Z * T
-
-    def o_send(j):
-        return remote(o_out.at[j], o_buf.at[h], o_s.at[j], o_r.at[h], at(f - 1, j, t))
-
-    def lo_send(j):
-        return remote(o_out.at[j], lo_buf, o_s.at[j], lo_r, at(h, j, t))
-
-    def attend(i, carry):
+    group = 2 if Z <= 4 else 1
+
+    def score(rows, slot):
+        return lax.dot_general(
+            rows,
+            kv_buf[slot, :, :, 0].reshape(keys_all, HD),
+            (((1,), (1,)), ((), ())),
+            preferred_element_type=jnp.float32,
+        )
+
+    def blend(weights, slot):
+        return jnp.dot(
+            weights.astype(jnp.bfloat16),
+            kv_buf[slot, :, :, 1].reshape(keys_all, HD),
+            preferred_element_type=jnp.float32,
+        )
+
+    def near(i, first):
         rows = q_buf[pl.ds(i * group, group)].reshape(group * T, HD)
-        scores = [
-            lax.dot_general(
-                rows,
-                kv_buf[slot, :, :, 0].reshape(keys_all, HD),
-                (((1,), (1,)), ((), ())),
-                preferred_element_type=jnp.float32,
-            )
-            for slot in range(3)
-        ]
-        highest = jnp.max(scores[0], axis=1, keepdims=True)
-        for slot in (1, 2):
-            highest = jnp.maximum(highest, jnp.max(scores[slot], axis=1, keepdims=True) - masks[slot])
-        total = jnp.zeros((group * T, 1), jnp.float32)
-        blended = jnp.zeros((group * T, HD), jnp.float32)
-        for slot in range(3):
-            weights = jnp.exp2((scores[slot] - (highest + masks[slot])) * rate)
-            total = total + jnp.sum(weights, axis=1, keepdims=True)
-            blended = blended + jnp.dot(
-                weights.astype(jnp.bfloat16),
-                kv_buf[slot, :, :, 1].reshape(keys_all, HD),
-                preferred_element_type=jnp.float32,
-            )
-        result = (blended / total).astype(jnp.bfloat16)
+        own = score(rows, 0)
+        if first:
+            for s in range(Z):
+                b = lax.rem(h + s, Z)
+                came(kv_buf.at[1, 1 - t, b], fwd_r.at[0, s])
+        beside = score(rows, 1)
+        highest = jnp.maximum(jnp.max(own, axis=1, keepdims=True), jnp.max(beside, axis=1, keepdims=True))
+        own = jnp.exp2((own - highest) * rate)
+        beside = jnp.exp2((beside - highest) * rate)
+        at_rows = pl.ds(i * group * T, group * T)
+        top[at_rows] = jnp.broadcast_to(highest, (group * T, HD))
+        total = jnp.sum(own, axis=1, keepdims=True) + jnp.sum(beside, axis=1, keepdims=True)
+        weight_sum[at_rows] = jnp.broadcast_to(total, (group * T, HD))
+        blended_buf[at_rows] = blend(own, 0) + blend(beside, 1)
+
+    if Z <= 4:
+        for i in range(Z // group):
+            for s in range(max(i * group, 1), (i + 1) * group):
+                came(q_buf.at[s], qz_r.at[s])
+            near(i, i == 0)
+    else:
+        for s in range(1, Z):
+            came(q_buf.at[s], qz_r.at[s])
+        near(0, True)
+        lax.fori_loop(1, Z // group, lambda i, c: (near(i, False), c)[1], 0)
+
+    @pl.when(has_across)
+    def _():
+        for s in range(Z):
+            b = lax.rem(h + Z - s, Z)
+            came(kv_buf.at[2, t, b], fr_r.at[1, s])
+            fwd_send(2, s, b).start()
+        for s in range(Z):
+            b = lax.rem(h + Z - s, Z)
+            came(kv_buf.at[2, 1 - t, b], fwd_r.at[1, s])
+
+    def o_send(s):
+        return remote(o_out.at[s], o_buf.at[h], o_s.at[s], o_r.at[h], at(f - 1, lax.rem(h + Z - s, Z), t))
+
+    def lo_send(s):
+        return remote(o_out.at[s], lo_buf, o_s.at[s], lo_r, at(h, lax.rem(h + Z - s, Z), t))
+
+    def leave_with(result, i):
         for g in range(group):
-            o_out[i * group + g] = result[g * T : (g + 1) * T]
-            j = i * group + g
+            s = i * group + g
+            o_out[s] = result[g * T : (g + 1) * T]
 
             @pl.when(f > 0)
             def _():
-                o_send(j).start()
-
-            @pl.when((f == 0) & ((h != 0) | (j != 0)))
-            def _():
-                lo_send(j).start()
-
-            @pl.when((f == 0) & (h == 0) & (j == 0))
+                o_send(s).start()
+
+            @pl.when((f == 0) & ((h != 0) | (s != 0)))
+            def _():
+                lo_send(s).start()
+
+            @pl.when((f == 0) & (h == 0) & (s == 0))
             def _():
                 pltpu.make_async_copy(o_out.at[0], lo_buf, lo_r).start()
 
+    def finish(i, carry):
+        at_rows = pl.ds(i * group * T, group * T)
+
+        @pl.when(has_across)
+        def _():
+            scores = score(q_buf[pl.ds(i * group, group)].reshape(group * T, HD), 2)
+            before = top[at_rows]
+            highest = jnp.maximum(before, jnp.max(scores, axis=1, keepdims=True))
+            keep = jnp.exp2((before - highest) * rate)
+            weights = jnp.exp2((scores - highest[:, 0:1]) * rate)
+            total = weight_sum[at_rows] * keep + jnp.sum(weights, axis=1, keepdims=True)
+            leave_with(((blended_buf[at_rows] * keep + blend(weights, 2)) / total).astype(jnp.bfloat16), i)
+
+        @pl.when(jnp.logical_not(has_across))
+        def _():
+            leave_with((blended_buf[at_rows] / weight_sum[at_rows]).astype(jnp.bfloat16), i)
+
         return carry
 
-    lax.fori_loop(0, Z // group, attend, 0)
+    if Z <= 4:
+        for i in range(Z // group):
+            finish(i, 0)
+    else:
+        lax.fori_loop(0, Z // group, finish, 0)
 
     @pl.when(f == F - 1)
     def _():
@@ -310,28 +319,24 @@
             kv_send(s).wait_send()
             q_send(s).wait_send()
         peer_send(s, 0, kv_out.at[0]).wait_send()
-
-        @pl.when(sends_next)
-        def _():
-            next_send(s, 0, kv_out.at[0]).wait_send()
-
-        @pl.when(sends_prev)
-        def _():
-            prev_send(s, 0, kv_out.at[0]).wait_send()
-
-        @pl.when(has_prev)
-        def _():
-            fwd_send(1, s, 0).wait_send()
-
-        @pl.when(has_next)
+        pair_send(s, 0, kv_out.at[0]).wait_send()
+        fwd_send(1, s, 0).wait_send()
+
+        @pl.when(has_across)
         def _():
             fwd_send(2, s, 0).wait_send()
 
         if relay:
 
-            @pl.when((f == 0) | (f == 3))
-            def _():
-                relay_down(s, 0).wait_send()
+            @pl.when(jnp.logical_not(has_across))
+            def _():
+                relay_send(s, 0).wait_send()
+
+        else:
+
+            @pl.when(has_across)
+            def _():
+                across_send(s, 0, kv_out.at[0]).wait_send()
 
         @pl.when((f > 0) | (h != 0) | (s != 0))
         def _():
@@ -388,16 +393,19 @@
                 pltpu.VMEM((8, HD), f32),
                 pltpu.VMEM((T, HH), bf),
                 pltpu.VMEM((T, HD), bf),
+                pltpu.VMEM((Z * T, HD), f32),
+                pltpu.VMEM((Z * T, HD), f32),
+                pltpu.VMEM((Z * T, HD), f32),
                 dma((3,)), dma((Z,)),
                 dma((Z,)), dma((Z,)), dma((Z,)), dma((Z,)),
-                dma((Z,)), dma((Z,)), dma((2, Z)), dma((2, Z)), dma((Z,)), dma((2, Z)), dma((2, Z)),
+                dma((Z,)), dma((Z,)), dma((2, Z)), dma((2, Z)), dma((2, Z)), dma((2, Z)),
                 dma((Z,)), dma((Z,)), dma,
                 dma, dma, dma((F,)), dma,
                 dma, dma, dma((F,)), dma,
                 dma((2,)),
             ],
             compiler_params=pltpu.CompilerParams(
-                collective_id=0, has_side_effects=True, vmem_limit_bytes=48 * 1024 * 1024
+                collective_id=0, has_side_effects=True, vmem_limit_bytes=60 * 1024 * 1024
             ),
         )(queries, keys, values, residual, incoming, gate_table, timesteps, positions)
 

time: 36.1 us -> 33.2 us (0.920)
  local copies, waits for them, and re-layouts: 6.6 us -> 2.16 us
  Pallas kernels: 27.2 us -> 28.9 us
    unnamed x14 -> x4, local copies, waits for them, and re-layouts: 6.6 us -> 2.16 us
    pallas_call x1, Pallas kernels: 27.2 us -> 28.9 us  [per_device(): pl.pallas_call(functools.partial(kernel, F, Z, F == 4), out_shape=(jax.Sh...]
where the time goes in v2:
time: 33.2 us; the launch traced here: 33 us
  Pallas kernels  28.9 us (87%)
  local copies, waits for them, and re-layouts  2.16 us (7%)
  between operations  1.94 us (6%)
    pallas_call x1, Pallas kernels, per_device(): pl.pallas_call(functools.partial(kernel, F, Z, F == 4), out_shape=(jax.Sh...  28.9 us
    unnamed x4, local copies, waits for them, and re-layouts  2.16 us

profile of v2, /device:TPU:0, one launch (start us, length us, event | category | flops | bytes accessed | tf_op | source)
XLA Modules:
  0.0 33.0 jit_solution(14904151920467809420)
XLA Ops:
  1.9 28.9 %shard_map.95 = (bf16[1,96,512]{2,1,0:T(8,128)(2,1)}, bf16[96,128]{1,0:T(8,128)(2,1)}) custom-call(bf16[1,96,512]{2,1,0:T(8,128)(2,1)} %q_hbm.1, bf16[1,96,512]{2,1,0:T(8,128)(2,1)} %k_hbm.1, bf16[1,96,512]{2,1,0:T(8,128)(2,1)} %v_hbm.1, bf16[1,96,512]{2,1,0:T(8,128)(2,1)} %res_hbm.1, bf16[96,512]{1,0:T(8,128)(2,1)} %inc_hbm.1, f32[50,512]{1,0:T(8,128)} %gate_hbm.1, ...), custom_call_target="tpu_custom_call" | custom-call | tf_op jit(solution)/shard_map/pallas_call | solution.py:370
  30.8 0.0 copy-start
  30.8 1.5 %copy.14 = bf16[1,96,512]{2,1,0:T(8,128)(2,1)} copy(bf16[1,96,512]{2,1,0:T(8,128)(2,1)} %get-tuple-element.4) | data formatting | bytes 196608
  32.4 0.0 copy-done
  32.4 0.6 %copy.15 = bf16[96,128]{1,0:T(8,128)(2,1)} copy(bf16[96,128]{1,0:T(8,128)(2,1)S(1)} %copy-done) | data formatting | bytes 49152
Async XLA Ops:
  30.8 1.6 %copy-start = (bf16[96,128]{1,0:T(8,128)(2,1)S(1)}, bf16[96,128]{1,0:T(8,128)(2,1)}, u32[]{:S(2)}) copy-start(bf16[96,128]{1,0:T(8,128)(2,1)} %get-tuple-element.5) | copy-start | bytes 73732

commit v3 on v2

v3 whole, which is shorter than its diff:
```python
import functools
import math

import jax
import jax.numpy as jnp
from jax import lax
from jax.experimental import pallas as pl
from jax.experimental.pallas import tpu as pltpu
from jax.sharding import PartitionSpec as P

HD = 128
HALF = 8
MESH = pl.DeviceIdType.MESH


def kernel(
    frames, heads, relay,
    q_hbm, k_hbm, v_hbm, res_hbm, inc_hbm, gate_hbm, steps_ref, pos_ref,
    nq_ref, lv_ref,
    q_in, k_in, gate_in, kv_out, q_out, gate_out,
    kv_buf, q_buf, o_out, o_buf, lo_buf, res_buf, lres_buf, gate_buf, lgate_buf,
    top, weight_sum, blended_buf,
    load_sem, v_sem, kvz_s, kvz_r, qz_s, qz_r, peer_s, peer_r, fr_s, fr_r, fwd_s, fwd_r,
    o_s, o_r, lo_r, res_s, res_r, lres_s, lres_r, gate_s, gate_r, lgate_s, lgate_r, out_sem,
):
    F, Z = frames, heads
    f = lax.axis_index("frame")
    h = lax.axis_index("head")
    t = lax.axis_index("tok")
    T = q_in.shape[0]
    has_prev = f > 0
    has_across = (f > 0) & (f < F - 1)
    partner = f + 1 - 2 * lax.rem(f, 2)
    across = f - 1 + 2 * lax.rem(f, 2)

    def at(fr, hd, tk):
        return {"frame": fr, "head": hd, "tok": tk}

    def remote(src, dst, send, recv, dev):
        return pltpu.make_async_remote_copy(
            src_ref=src, dst_ref=dst, send_sem=send, recv_sem=recv, device_id=dev, device_id_type=MESH
        )

    load_k = pltpu.make_async_copy(k_hbm.at[0], k_in, load_sem.at[0])
    load_q = pltpu.make_async_copy(q_hbm.at[0], q_in, load_sem.at[1])
    load_gate = pltpu.make_async_copy(gate_hbm, gate_in, load_sem.at[2])
    load_v = [
        pltpu.make_async_copy(v_hbm.at[0, :, pl.ds(j * HD, HD)], kv_out.at[j, 1], v_sem.at[j]) for j in range(Z)
    ]
    incoming = pltpu.make_async_copy(inc_hbm, nq_ref.at[0], out_sem)
    load_q.start()
    load_k.start()
    for c in load_v:
        c.start()
    load_gate.start()

    @pl.when(f == F - 1)
    def _():
        incoming.start()

    barrier = pltpu.get_barrier_semaphore()
    me = f * Z + h

    def greet(s, carry):
        other = lax.rem(me + s, F * Z)
        pl.semaphore_signal(barrier, inc=1, device_id=at(other // Z, lax.rem(other, Z), t), device_id_type=MESH)
        return carry

    lax.fori_loop(1, F * Z, greet, 0)
    pl.semaphore_signal(barrier, inc=1, device_id=at(f, h, 1 - t), device_id_type=MESH)

    lane = lax.broadcasted_iota(jnp.int32, (8, HD), 1)
    power = lax.rem(lane, HALF).astype(jnp.float32)
    angle = pos_ref[0].astype(jnp.float32) * jnp.exp2(-power)
    cosine = jnp.where(lane < 2 * HALF, jnp.cos(angle), 1.0)[0:1]
    sine = jnp.sin(angle)
    sine_up = jnp.where(lane < HALF, -sine, 0.0)[0:1]
    sine_down = jnp.where((lane >= HALF) & (lane < 2 * HALF), sine, 0.0)[0:1]

    def turned(x):
        x = x.astype(jnp.float32)
        up = pltpu.roll(x, HD - HALF, 1)
        down = pltpu.roll(x, HALF, 1)
        return (x * cosine + up * sine_up + down * sine_down).astype(jnp.bfloat16)

    load_q.wait()
    for j in range(Z):
        q_out[j] = turned(q_in[:, j * HD : (j + 1) * HD])
    load_k.wait()
    for j in range(Z):
        kv_out[j, 0] = turned(k_in[:, j * HD : (j + 1) * HD])
    for c in load_v:
        c.wait()
    pl.semaphore_wait(barrier, F * Z)

    def q_send(s):
        return remote(q_out.at[lax.rem(h + s, Z)], q_buf.at[s], qz_s.at[s], qz_r.at[s], at(f, lax.rem(h + s, Z), t))

    def kv_send(s):
        d = lax.rem(h + s, Z)
        return remote(kv_out.at[d], kv_buf.at[0, s, t], kvz_s.at[s], kvz_r.at[s], at(f, d, t))

    for s in range(1, Z):
        q_send(s).start()
    for s in range(1, Z):
        kv_send(s).start()

    def peer_send(s, src):
        return remote(src, kv_buf.at[0, s, t], peer_s.at[s], peer_r.at[s], at(f, h, 1 - t))

    def pair_send(s, src):
        return remote(src, kv_buf.at[1, s, t], fr_s.at[0, s], fr_r.at[0, s], at(partner, h, t))

    def across_send(s, src):
        return remote(src, kv_buf.at[2, s, t], fr_s.at[1, s], fr_r.at[1, s], at(across, h, t))

    def relay_send(s):
        return remote(
            kv_buf.at[1, s, t], kv_buf.at[2, s, t], fr_s.at[1, s], fr_r.at[1, s], at(lax.rem(f + 2, F), h, t)
        )

    def fwd_send(slot, s):
        ref = kv_buf.at[slot, s, t]
        return remote(ref, ref, fwd_s.at[slot - 1, s], fwd_r.at[slot - 1, s], at(f, h, 1 - t))

    def spread(s, src):
        pair_send(s, src).start()
        if not relay:

            @pl.when(has_across)
            def _():
                across_send(s, src).start()

        peer_send(s, src).start()

    spread(0, kv_out.at[h])
    kv_buf[0, 0, t] = kv_out[h]
    q_buf[0] = q_out[h]

    load_gate.wait()
    gate_out[...] = jnp.broadcast_to(gate_in[pl.ds(steps_ref[0], 1), :], gate_out.shape)

    def came(ref, sem):
        remote(ref, ref, sem, sem, at(f, h, 1 - t)).wait_recv()

    def take_own(s):
        came(kv_buf.at[0, s, t], kvz_r.at[s])
        spread(s, kv_buf.at[0, s, t])

    def take_pair(s):
        came(kv_buf.at[1, s, t], fr_r.at[0, s])
        if relay:

            @pl.when(jnp.logical_not(has_across))
            def _():
                relay_send(s).start()

        fwd_send(1, s).start()

    def take_across(s):
        @pl.when(has_across)
        def _():
            came(kv_buf.at[2, s, t], fr_r.at[1, s])
            fwd_send(2, s).start()

    def res_send():
        return remote(res_hbm, res_buf, res_s, res_r, at(f - 1, h, t))

    def gate_send():
        return remote(gate_out, gate_buf, gate_s, gate_r, at(f - 1, h, t))

    def lres_send(g):
        return remote(res_hbm.at[0, :, pl.ds(g * HD, HD)], lres_buf, lres_s.at[g], lres_r, at(g, h, t))

    def lgate_send(g):
        return remote(gate_out.at[:, pl.ds(g * HD, HD)], lgate_buf, lgate_s.at[g], lgate_r, at(g, h, t))

    def send_residual():
        @pl.when(has_prev)
        def _():
            res_send().start()
            gate_send().start()

        @pl.when(f == 0)
        def _():
            pltpu.make_async_copy(res_hbm.at[0, :, pl.ds(0, HD)], lres_buf, lres_r).start()
            pltpu.make_async_copy(gate_out.at[:, pl.ds(0, HD)], lgate_buf, lgate_r).start()
            for g in range(1, F):
                lres_send(g).start()
                lgate_send(g).start()

    rate = math.log2(math.e) / math.sqrt(HD)

    def merged(i, blocks, parts, first):
        rows = q_buf[pl.ds(i, blocks)].reshape(blocks * T, HD)
        at_rows = pl.ds(i * T, blocks * T)
        near_keys = jnp.concatenate([kv_buf[p, s, :, 0].reshape(2 * T, HD) for p, s in parts])
        near_values = jnp.concatenate([kv_buf[p, s, :, 1].reshape(2 * T, HD) for p, s in parts])
        scores = lax.dot_general(rows, near_keys, (((1,), (1,)), ((), ())), preferred_element_type=jnp.float32)
        highest = jnp.max(scores, axis=1, keepdims=True)
        if not first:
            before = top[at_rows]
            highest = jnp.maximum(before, highest)
            keep = jnp.exp2((before - highest) * rate)
        weights = jnp.exp2((scores - highest[:, 0:1]) * rate)
        total = jnp.sum(weights, axis=1, keepdims=True)
        blended = jnp.dot(weights.astype(jnp.bfloat16), near_values, preferred_element_type=jnp.float32)
        if not first:
            total = weight_sum[at_rows] * keep + total
            blended = blended_buf[at_rows] * keep + blended
        return highest, total, blended

    def gather(parts, first):
        blocks = min(Z, 4)

        def step(i, carry):
            highest, total, blended = merged(i * blocks, blocks, parts, first)
            at_rows = pl.ds(i * blocks * T, blocks * T)
            top[at_rows] = jnp.broadcast_to(highest, (blocks * T, HD))
            weight_sum[at_rows] = jnp.broadcast_to(total, (blocks * T, HD))
            blended_buf[at_rows] = blended
            return carry

        if Z == blocks:
            step(0, 0)
        else:
            lax.fori_loop(0, Z // blocks, step, 0)

    def near(s):
        came(kv_buf.at[0, s, 1 - t], peer_r.at[s])
        came(kv_buf.at[1, s, 1 - t], fwd_r.at[0, s])
        gather([(0, s), (1, s)], s == 0)

    def wait_across(s):
        for p in (s, s + 1):
            came(kv_buf.at[2, p, 1 - t], fwd_r.at[1, p])

    def far(s):
        @pl.when(has_across)
        def _():
            wait_across(s)
            gather([(2, s), (2, s + 1)], False)

    for s in range(Z):
        if s + 1 < Z:
            take_own(s + 1)
        take_pair(s)
        if s == Z - 1:
            send_residual()
        if s == 1:
            for p in range(1, Z):
                came(q_buf.at[p], qz_r.at[p])
        if s >= 1:
            near(s - 1)
        if s >= 2:
            take_across(s - 2)
        if s >= 3 and s % 2 == 1:
            far(s - 3)
    take_across(Z - 2)
    near(Z - 1)

    def o_send(s):
        return remote(o_out.at[s], o_buf.at[h], o_s.at[s], o_r.at[h], at(f - 1, lax.rem(h + Z - s, Z), t))

    def lo_send(s):
        return remote(o_out.at[s], lo_buf, o_s.at[s], lo_r, at(h, lax.rem(h + Z - s, Z), t))

    group = 2

    def leave_with(blended, total, i):
        result = (blended / total).astype(jnp.bfloat16)
        for g in range(group):
            s = i * group + g
            o_out[s] = result[g * T : (g + 1) * T]

            @pl.when(f > 0)
            def _():
                o_send(s).start()

            @pl.when((f == 0) & ((h != 0) | (s != 0)))
            def _():
                lo_send(s).start()

            @pl.when((f == 0) & (h == 0) & (s == 0))
            def _():
                pltpu.make_async_copy(o_out.at[0], lo_buf, lo_r).start()

    def each_group(body):
        if Z <= 4:
            for i in range(Z // group):
                body(i, 0)
        else:
            lax.fori_loop(0, Z // group, body, 0)

    @pl.when(has_across)
    def _():
        came(kv_buf.at[2, Z - 1, t], fr_r.at[1, Z - 1])
        fwd_send(2, Z - 1).start()
        wait_across(Z - 2)

        def last(i, carry):
            _, total, blended = merged(i * group, group, [(2, Z - 2), (2, Z - 1)], False)
            leave_with(blended, total, i)
            return carry

        each_group(last)

    @pl.when(jnp.logical_not(has_across))
    def _():
        def last(i, carry):
            at_rows = pl.ds(i * group * T, group * T)
            leave_with(blended_buf[at_rows], weight_sum[at_rows], i)
            return carry

        each_group(last)

    came(lres_buf, lres_r)
    came(lgate_buf, lgate_r)
    came(lo_buf, lo_r)
    lv_ref[...] = (
        lres_buf[...].astype(jnp.float32) + lgate_buf[0:1, :] * lo_buf[...].astype(jnp.float32)
    ).astype(jnp.bfloat16)

    @pl.when(f < F - 1)
    def _():
        came(res_buf, res_r)
        came(gate_buf, gate_r)
        for j in range(Z):
            came(o_buf.at[j], o_r.at[j])
            cols = slice(j * HD, (j + 1) * HD)
            nq_ref[0, :, cols] = (
                res_buf[0, :, cols].astype(jnp.float32) + gate_buf[0:1, cols] * o_buf[j].astype(jnp.float32)
            ).astype(jnp.bfloat16)

    @pl.when(f == F - 1)
    def _():
        incoming.wait()

    for s in range(Z):
        if s > 0:
            kv_send(s).wait_send()
            q_send(s).wait_send()
        peer_send(s, kv_out.at[0]).wait_send()
        pair_send(s, kv_out.at[0]).wait_send()
        fwd_send(1, s).wait_send()

        @pl.when(has_across)
        def _():
            fwd_send(2, s).wait_send()

        if relay:

            @pl.when(jnp.logical_not(has_across))
            def _():
                relay_send(s).wait_send()

        else:

            @pl.when(has_across)
            def _():
                across_send(s, kv_out.at[0]).wait_send()

        @pl.when((f > 0) | (h != 0) | (s != 0))
        def _():
            o_send(s).wait_send()

    @pl.when(has_prev)
    def _():
        res_send().wait_send()
        gate_send().wait_send()

    @pl.when(f == 0)
    def _():
        for g in range(1, F):
            lres_send(g).wait_send()
            lgate_send(g).wait_send()


def solution(mesh):
    F, Z = mesh.shape["frame"], mesh.shape["head"]

    def per_device(queries, keys, values, residual, incoming, gate_table, timesteps, positions):
        T, HH = queries.shape[1], queries.shape[2]
        assert HH == Z * HD and HH == F * HD and mesh.shape["tok"] == 2
        blocks = (queries, keys, values, residual, incoming, gate_table)
        bf, f32 = jnp.bfloat16, jnp.float32
        dma = pltpu.SemaphoreType.DMA
        anywhere = pl.BlockSpec(memory_space=pl.ANY)
        smem = pl.BlockSpec(memory_space=pltpu.SMEM)
        return pl.pallas_call(
            functools.partial(kernel, F, Z, F == 4),
            out_shape=(
                jax.ShapeDtypeStruct((1, T, HH), bf),
                jax.ShapeDtypeStruct((T, HD), bf),
            ),
            in_specs=[anywhere] * 6 + [smem, smem],
            out_specs=(pl.BlockSpec(memory_space=pltpu.VMEM),) * 2,
            scratch_shapes=[
                pltpu.VMEM((T, HH), bf),
                pltpu.VMEM((T, HH), bf),
                pltpu.VMEM(gate_table.shape, f32),
                pltpu.VMEM((Z, 2, T, HD), bf),
                pltpu.VMEM((Z, T, HD), bf),
                pltpu.VMEM((8, HH), f32),
                pltpu.VMEM((3, Z, 2, 2, T, HD), bf),
                pltpu.VMEM((Z, T, HD), bf),
                pltpu.VMEM((Z, T, HD), bf),
                pltpu.VMEM((Z, T, HD), bf),
                pltpu.VMEM((T, HD), bf),
                pltpu.VMEM((1, T, HH), bf),
                pltpu.VMEM((T, HD), bf),
                pltpu.VMEM((8, HH), f32),
                pltpu.VMEM((8, HD), f32),
                pltpu.VMEM((Z * T, HD), f32),
                pltpu.VMEM((Z * T, HD), f32),
                pltpu.VMEM((Z * T, HD), f32),
                dma((3,)), dma((Z,)),
                dma((Z,)), dma((Z,)), dma((Z,)), dma((Z,)),
                dma((Z,)), dma((Z,)), dma((2, Z)), dma((2, Z)), dma((2, Z)), dma((2, Z)),
                dma((Z,)), dma((Z,)), dma,
                dma, dma, dma((F,)), dma,
                dma, dma, dma((F,)), dma,
                dma,
            ],
            compiler_params=pltpu.CompilerParams(
                collective_id=0, has_side_effects=True, vmem_limit_bytes=48 * 1024 * 1024
            ),
        )(
            *(pltpu.with_memory_space_constraint(x, pltpu.HBM) for x in blocks), timesteps, positions
        )

    placed = (
        P("frame", ("head", "tok"), None),
        P("frame", ("head", "tok"), None),
        P("frame", ("head", "tok"), None),
        P("frame", ("head", "tok"), None),
        P(("head", "tok"), None),
        P(),
        P("frame"),
        P("frame"),
    )
    return jax.shard_map(
        per_device,
        mesh=mesh,
        in_specs=placed,
        out_specs=(P("frame", ("head", "tok"), None), P(("head", "tok"), "frame")),
        check_vma=False,
    )
```

time: 33.2 us -> 33.8 us (1.018)
  Pallas kernels: 28.9 us -> 30.4 us
  local copies, waits for them, and re-layouts: 2.16 us -> 1.25 us
    pallas_call x1, Pallas kernels: 28.9 us -> 30.4 us  [per_device(): pl.pallas_call(functools.partial(kernel, F, Z, F == 4), out_shape=(jax.Sh...]
    unnamed x4 -> x2, local copies, waits for them, and re-layouts: 2.16 us -> 1.25 us
where the time goes in v3:
time: 33.8 us; the launch traced here: 33.6 us
  Pallas kernels  30.4 us (90%)
  between operations  1.93 us (6%)
  local copies, waits for them, and re-layouts  1.25 us (4%)
    pallas_call x1, Pallas kernels, per_device(): pl.pallas_call(functools.partial(kernel, F, Z, F == 4), out_shape=(jax.Sh...  30.4 us
    unnamed x2, local copies, waits for them, and re-layouts  1.25 us

profile of v3, /device:TPU:0, one launch (start us, length us, event | category | flops | bytes accessed | tf_op | source)
XLA Modules:
  0.0 33.6 jit_solution(14376777687289343888)
XLA Ops:
  1.9 30.4 %shard_map.95 = (bf16[1,96,512]{2,1,0:T(8,128)(2,1)S(1)}, bf16[96,128]{1,0:T(8,128)(2,1)S(1)}) custom-call(bf16[1,96,512]{2,1,0:T(8,128)(2,1)} %q_hbm.1, bf16[1,96,512]{2,1,0:T(8,128)(2,1)} %k_hbm.1, bf16[1,96,512]{2,1,0:T(8,128)(2,1)} %v_hbm.1, bf16[1,96,512]{2,1,0:T(8,128)(2,1)} %res_hbm.1, bf16[96,512]{1,0:T(8,128)(2,1)} %inc_hbm.1, f32[50,512]{1,0:T(8,128)} %gate_hbm.1, ...), custom_call_target="tpu_custom_call" | custom-call | tf_op jit(solution)/shard_map/pallas_call | solution.py:390
  32.4 0.6 %copy.14 = bf16[1,96,512]{2,1,0:T(8,128)(2,1)} copy(bf16[1,96,512]{2,1,0:T(8,128)(2,1)S(1)} %get-tuple-element.4) | data formatting | bytes 196608
  33.0 0.6 %copy.15 = bf16[96,128]{1,0:T(8,128)(2,1)} copy(bf16[96,128]{1,0:T(8,128)(2,1)S(1)} %get-tuple-element.5) | data formatting | bytes 49152

commit v4 on v3

--- a/solution.py
+++ b/solution.py
@@ -19,7 +19,7 @@
     nq_ref, lv_ref,
     q_in, k_in, gate_in, kv_out, q_out, gate_out,
     kv_buf, q_buf, o_out, o_buf, lo_buf, res_buf, lres_buf, gate_buf, lgate_buf,
-    top, weight_sum, blended_buf,
+    q_cols, top, weight_sum, blended_buf,
     load_sem, v_sem, kvz_s, kvz_r, qz_s, qz_r, peer_s, peer_r, fr_s, fr_r, fwd_s, fwd_r,
     o_s, o_r, lo_r, res_s, res_r, lres_s, lres_r, gate_s, gate_r, lgate_s, lgate_r, out_sem,
 ):
@@ -190,41 +190,54 @@
                 lgate_send(g).start()
 
     rate = math.log2(math.e) / math.sqrt(HD)
-
-    def merged(i, blocks, parts, first):
-        rows = q_buf[pl.ds(i, blocks)].reshape(blocks * T, HD)
-        at_rows = pl.ds(i * T, blocks * T)
-        near_keys = jnp.concatenate([kv_buf[p, s, :, 0].reshape(2 * T, HD) for p, s in parts])
-        near_values = jnp.concatenate([kv_buf[p, s, :, 1].reshape(2 * T, HD) for p, s in parts])
-        scores = lax.dot_general(rows, near_keys, (((1,), (1,)), ((), ())), preferred_element_type=jnp.float32)
-        highest = jnp.max(scores, axis=1, keepdims=True)
+    group = min(Z, 4)
+    width = group * T
+
+    def columns(i):
+        return pl.ds(i * width, width)
+
+    def turn_queries(i, carry):
+        rows = q_buf[pl.ds(i * group, group)].reshape(width, HD)
+        q_cols[:, columns(i)] = rows.T
+        return carry
+
+    def merged(i, keys, values, first):
+        scores = jnp.dot(keys, q_cols[:, columns(i)], preferred_element_type=jnp.float32)
+        highest = jnp.max(scores, axis=0, keepdims=True)
         if not first:
-            before = top[at_rows]
+            before = top[0:1, columns(i)]
             highest = jnp.maximum(before, highest)
             keep = jnp.exp2((before - highest) * rate)
-        weights = jnp.exp2((scores - highest[:, 0:1]) * rate)
-        total = jnp.sum(weights, axis=1, keepdims=True)
-        blended = jnp.dot(weights.astype(jnp.bfloat16), near_values, preferred_element_type=jnp.float32)
+        weights = jnp.exp2((scores - highest) * rate)
+        total = jnp.sum(weights, axis=0, keepdims=True)
+        blended = jnp.dot(values, weights.astype(jnp.bfloat16), preferred_element_type=jnp.float32)
         if not first:
-            total = weight_sum[at_rows] * keep + total
-            blended = blended_buf[at_rows] * keep + blended
+            total = weight_sum[0:1, columns(i)] * keep + total
+            blended = blended_buf[:, columns(i)] * keep + blended
         return highest, total, blended
 
+    def block_pair(parts):
+        keys = jnp.concatenate([kv_buf[p, s, :, 0].reshape(2 * T, HD) for p, s in parts])
+        values = jnp.concatenate([kv_buf[p, s, :, 1].reshape(2 * T, HD) for p, s in parts])
+        return keys, values.T
+
+    def each_group(body):
+        if Z == group:
+            body(0, 0)
+        else:
+            lax.fori_loop(0, Z // group, body, 0)
+
     def gather(parts, first):
-        blocks = min(Z, 4)
+        keys, values = block_pair(parts)
 
         def step(i, carry):
-            highest, total, blended = merged(i * blocks, blocks, parts, first)
-            at_rows = pl.ds(i * blocks * T, blocks * T)
-            top[at_rows] = jnp.broadcast_to(highest, (blocks * T, HD))
-            weight_sum[at_rows] = jnp.broadcast_to(total, (blocks * T, HD))
-            blended_buf[at_rows] = blended
+            highest, total, blended = merged(i, keys, values, first)
+            top[0:1, columns(i)] = highest
+            weight_sum[0:1, columns(i)] = total
+            blended_buf[:, columns(i)] = blended
             return carry
 
-        if Z == blocks:
-            step(0, 0)
-        else:
-            lax.fori_loop(0, Z // blocks, step, 0)
+        each_group(step)
 
     def near(s):
         came(kv_buf.at[0, s, 1 - t], peer_r.at[s])
@@ -250,6 +263,7 @@
         if s == 1:
             for p in range(1, Z):
                 came(q_buf.at[p], qz_r.at[p])
+            each_group(turn_queries)
         if s >= 1:
             near(s - 1)
         if s >= 2:
@@ -265,10 +279,8 @@
     def lo_send(s):
         return remote(o_out.at[s], lo_buf, o_s.at[s], lo_r, at(h, lax.rem(h + Z - s, Z), t))
 
-    group = 2
-
     def leave_with(blended, total, i):
-        result = (blended / total).astype(jnp.bfloat16)
+        result = (blended / total).T.astype(jnp.bfloat16)
         for g in range(group):
             s = i * group + g
             o_out[s] = result[g * T : (g + 1) * T]
@@ -285,21 +297,15 @@
             def _():
                 pltpu.make_async_copy(o_out.at[0], lo_buf, lo_r).start()
 
-    def each_group(body):
-        if Z <= 4:
-            for i in range(Z // group):
-                body(i, 0)
-        else:
-            lax.fori_loop(0, Z // group, body, 0)
-
     @pl.when(has_across)
     def _():
         came(kv_buf.at[2, Z - 1, t], fr_r.at[1, Z - 1])
         fwd_send(2, Z - 1).start()
         wait_across(Z - 2)
+        keys, values = block_pair([(2, Z - 2), (2, Z - 1)])
 
         def last(i, carry):
-            _, total, blended = merged(i * group, group, [(2, Z - 2), (2, Z - 1)], False)
+            _, total, blended = merged(i, keys, values, False)
             leave_with(blended, total, i)
             return carry
 
@@ -308,8 +314,7 @@
     @pl.when(jnp.logical_not(has_across))
     def _():
         def last(i, carry):
-            at_rows = pl.ds(i * group * T, group * T)
-            leave_with(blended_buf[at_rows], weight_sum[at_rows], i)
+            leave_with(blended_buf[:, columns(i)], weight_sum[0:1, columns(i)], i)
             return carry
 
         each_group(last)
@@ -411,9 +416,10 @@
                 pltpu.VMEM((T, HD), bf),
                 pltpu.VMEM((8, HH), f32),
                 pltpu.VMEM((8, HD), f32),
-                pltpu.VMEM((Z * T, HD), f32),
-                pltpu.VMEM((Z * T, HD), f32),
-                pltpu.VMEM((Z * T, HD), f32),
+                pltpu.VMEM((HD, Z * T), bf),
+                pltpu.VMEM((8, Z * T), f32),
+                pltpu.VMEM((8, Z * T), f32),
+                pltpu.VMEM((HD, Z * T), f32),
                 dma((3,)), dma((Z,)),
                 dma((Z,)), dma((Z,)), dma((Z,)), dma((Z,)),
                 dma((Z,)), dma((Z,)), dma((2, Z)), dma((2, Z)), dma((2, Z)), dma((2, Z)),

time: 33.8 us -> 33.7 us (level)
  no operation moved by 1% of the time
where the time goes in v4:
time: 33.7 us; the launch traced here: 33.5 us
  Pallas kernels  30.3 us (90%)
  between operations  1.93 us (6%)
  local copies, waits for them, and re-layouts  1.25 us (4%)
    pallas_call x1, Pallas kernels, per_device(): pl.pallas_call(functools.partial(kernel, F, Z, F == 4), out_shape=(jax.Sh...  30.3 us
    unnamed x2, local copies, waits for them, and re-layouts  1.25 us

profile of v4, /device:TPU:0, one launch (start us, length us, event | category | flops | bytes accessed | tf_op | source)
XLA Modules:
  0.0 33.5 jit_solution(12593996527500053204)
XLA Ops:
  1.9 30.3 %shard_map.95 = (bf16[1,96,512]{2,1,0:T(8,128)(2,1)S(1)}, bf16[96,128]{1,0:T(8,128)(2,1)S(1)}) custom-call(bf16[1,96,512]{2,1,0:T(8,128)(2,1)} %q_hbm.1, bf16[1,96,512]{2,1,0:T(8,128)(2,1)} %k_hbm.1, bf16[1,96,512]{2,1,0:T(8,128)(2,1)} %v_hbm.1, bf16[1,96,512]{2,1,0:T(8,128)(2,1)} %res_hbm.1, bf16[96,512]{1,0:T(8,128)(2,1)} %inc_hbm.1, f32[50,512]{1,0:T(8,128)} %gate_hbm.1, ...), custom_call_target="tpu_custom_call" | custom-call | tf_op jit(solution)/shard_map/pallas_call | solution.py:395
  32.2 0.6 %copy.14 = bf16[1,96,512]{2,1,0:T(8,128)(2,1)} copy(bf16[1,96,512]{2,1,0:T(8,128)(2,1)S(1)} %get-tuple-element.4) | data formatting | bytes 196608
  32.9 0.6 %copy.15 = bf16[96,128]{1,0:T(8,128)(2,1)} copy(bf16[96,128]{1,0:T(8,128)(2,1)S(1)} %get-tuple-element.5) | data formatting | bytes 49152

commit v5 on v4

--- a/solution.py
+++ b/solution.py
@@ -19,8 +19,8 @@
     nq_ref, lv_ref,
     q_in, k_in, gate_in, kv_out, q_out, gate_out,
     kv_buf, q_buf, o_out, o_buf, lo_buf, res_buf, lres_buf, gate_buf, lgate_buf,
-    q_cols, top, weight_sum, blended_buf,
-    load_sem, v_sem, kvz_s, kvz_r, qz_s, qz_r, peer_s, peer_r, fr_s, fr_r, fwd_s, fwd_r,
+    q_cols, stats, blended_buf, other_stats, other_blended,
+    load_sem, v_sem, kvz_s, kvz_r, qz_s, qz_r, peer_s, peer_r, fr_s, fr_r, part_s, part_r,
     o_s, o_r, lo_r, res_s, res_r, lres_s, lres_r, gate_s, gate_r, lgate_s, lgate_r, out_sem,
 ):
     F, Z = frames, heads
@@ -94,11 +94,11 @@
     pl.semaphore_wait(barrier, F * Z)
 
     def q_send(s):
-        return remote(q_out.at[lax.rem(h + s, Z)], q_buf.at[s], qz_s.at[s], qz_r.at[s], at(f, lax.rem(h + s, Z), t))
+        return remote(q_out.at[lax.rem(h + s, Z)], q_buf.at[0, s], qz_s.at[s], qz_r.at[s], at(f, lax.rem(h + s, Z), t))
 
     def kv_send(s):
         d = lax.rem(h + s, Z)
-        return remote(kv_out.at[d], kv_buf.at[0, s, t], kvz_s.at[s], kvz_r.at[s], at(f, d, t))
+        return remote(kv_out.at[d], kv_buf.at[0, s], kvz_s.at[s], kvz_r.at[s], at(f, d, t))
 
     for s in range(1, Z):
         q_send(s).start()
@@ -106,22 +106,16 @@
         kv_send(s).start()
 
     def peer_send(s, src):
-        return remote(src, kv_buf.at[0, s, t], peer_s.at[s], peer_r.at[s], at(f, h, 1 - t))
+        return remote(src, q_buf.at[1, s], peer_s.at[s], peer_r.at[s], at(f, h, 1 - t))
 
     def pair_send(s, src):
-        return remote(src, kv_buf.at[1, s, t], fr_s.at[0, s], fr_r.at[0, s], at(partner, h, t))
+        return remote(src, kv_buf.at[1, s], fr_s.at[0, s], fr_r.at[0, s], at(partner, h, t))
 
     def across_send(s, src):
-        return remote(src, kv_buf.at[2, s, t], fr_s.at[1, s], fr_r.at[1, s], at(across, h, t))
+        return remote(src, kv_buf.at[2, s], fr_s.at[1, s], fr_r.at[1, s], at(across, h, t))
 
     def relay_send(s):
-        return remote(
-            kv_buf.at[1, s, t], kv_buf.at[2, s, t], fr_s.at[1, s], fr_r.at[1, s], at(lax.rem(f + 2, F), h, t)
-        )
-
-    def fwd_send(slot, s):
-        ref = kv_buf.at[slot, s, t]
-        return remote(ref, ref, fwd_s.at[slot - 1, s], fwd_r.at[slot - 1, s], at(f, h, 1 - t))
+        return remote(kv_buf.at[1, s], kv_buf.at[2, s], fr_s.at[1, s], fr_r.at[1, s], at(lax.rem(f + 2, F), h, t))
 
     def spread(s, src):
         pair_send(s, src).start()
@@ -131,11 +125,10 @@
             def _():
                 across_send(s, src).start()
 
-        peer_send(s, src).start()
-
     spread(0, kv_out.at[h])
-    kv_buf[0, 0, t] = kv_out[h]
-    q_buf[0] = q_out[h]
+    peer_send(0, q_out.at[h]).start()
+    kv_buf[0, 0] = kv_out[h]
+    q_buf[0, 0] = q_out[h]
 
     load_gate.wait()
     gate_out[...] = jnp.broadcast_to(gate_in[pl.ds(steps_ref[0], 1), :], gate_out.shape)
@@ -143,25 +136,21 @@
     def came(ref, sem):
         remote(ref, ref, sem, sem, at(f, h, 1 - t)).wait_recv()
 
+    def take_queries(s):
+        came(q_buf.at[0, s], qz_r.at[s])
+        peer_send(s, q_buf.at[0, s]).start()
+
     def take_own(s):
-        came(kv_buf.at[0, s, t], kvz_r.at[s])
-        spread(s, kv_buf.at[0, s, t])
+        came(kv_buf.at[0, s], kvz_r.at[s])
+        spread(s, kv_buf.at[0, s])
 
     def take_pair(s):
-        came(kv_buf.at[1, s, t], fr_r.at[0, s])
+        came(kv_buf.at[1, s], fr_r.at[0, s])
         if relay:
 
             @pl.when(jnp.logical_not(has_across))
             def _():
                 relay_send(s).start()
-
-        fwd_send(1, s).start()
-
-    def take_across(s):
-        @pl.when(has_across)
-        def _():
-            came(kv_buf.at[2, s, t], fr_r.at[1, s])
-            fwd_send(2, s).start()
 
     def res_send():
         return remote(res_hbm, res_buf, res_s, res_r, at(f - 1, h, t))
@@ -197,28 +186,31 @@
         return pl.ds(i * width, width)
 
     def turn_queries(i, carry):
-        rows = q_buf[pl.ds(i * group, group)].reshape(width, HD)
-        q_cols[:, columns(i)] = rows.T
+        for half in range(2):
+            rows = q_buf[half, pl.ds(i * group, group)].reshape(width, HD)
+            q_cols[half, :, columns(i)] = rows.T
         return carry
 
-    def merged(i, keys, values, first):
-        scores = jnp.dot(keys, q_cols[:, columns(i)], preferred_element_type=jnp.float32)
+    def merged(i, half, keys, values, first):
+        scores = jnp.dot(keys, q_cols[half, :, columns(i)], preferred_element_type=jnp.float32)
         highest = jnp.max(scores, axis=0, keepdims=True)
         if not first:
-            before = top[0:1, columns(i)]
+            before = stats[half, 0, 0:1, columns(i)]
             highest = jnp.maximum(before, highest)
             keep = jnp.exp2((before - highest) * rate)
         weights = jnp.exp2((scores - highest) * rate)
         total = jnp.sum(weights, axis=0, keepdims=True)
         blended = jnp.dot(values, weights.astype(jnp.bfloat16), preferred_element_type=jnp.float32)
         if not first:
-            total = weight_sum[0:1, columns(i)] * keep + total
-            blended = blended_buf[:, columns(i)] * keep + blended
-        return highest, total, blended
+            total = stats[half, 1, 0:1, columns(i)] * keep + total
+            blended = blended_buf[half, :, columns(i)] * keep + blended
+        stats[half, 0, :, columns(i)] = jnp.broadcast_to(highest, (8, width))
+        stats[half, 1, :, columns(i)] = jnp.broadcast_to(total, (8, width))
+        blended_buf[half, :, columns(i)] = blended
 
     def block_pair(parts):
-        keys = jnp.concatenate([kv_buf[p, s, :, 0].reshape(2 * T, HD) for p, s in parts])
-        values = jnp.concatenate([kv_buf[p, s, :, 1].reshape(2 * T, HD) for p, s in parts])
+        keys = jnp.concatenate([kv_buf[p, s, 0] for p, s in parts])
+        values = jnp.concatenate([kv_buf[p, s, 1] for p, s in parts])
         return keys, values.T
 
     def each_group(body):
@@ -227,51 +219,43 @@
         else:
             lax.fori_loop(0, Z // group, body, 0)
 
-    def gather(parts, first):
+    def gather(parts, first, between=None):
         keys, values = block_pair(parts)
-
-        def step(i, carry):
-            highest, total, blended = merged(i, keys, values, first)
-            top[0:1, columns(i)] = highest
-            weight_sum[0:1, columns(i)] = total
-            blended_buf[:, columns(i)] = blended
-            return carry
-
-        each_group(step)
-
-    def near(s):
-        came(kv_buf.at[0, s, 1 - t], peer_r.at[s])
-        came(kv_buf.at[1, s, 1 - t], fwd_r.at[0, s])
-        gather([(0, s), (1, s)], s == 0)
-
-    def wait_across(s):
-        for p in (s, s + 1):
-            came(kv_buf.at[2, p, 1 - t], fwd_r.at[1, p])
-
-    def far(s):
-        @pl.when(has_across)
-        def _():
-            wait_across(s)
-            gather([(2, s), (2, s + 1)], False)
+        for half in (1, 0):
+
+            def step(i, carry):
+                merged(i, half, keys, values, first)
+                return carry
+
+            each_group(step)
+            if half == 1 and between is not None:
+                between()
 
     for s in range(Z):
+        take_pair(s)
+        if s == 0:
+            for p in range(1, Z):
+                take_queries(p)
         if s + 1 < Z:
             take_own(s + 1)
-        take_pair(s)
         if s == Z - 1:
             send_residual()
         if s == 1:
-            for p in range(1, Z):
-                came(q_buf.at[p], qz_r.at[p])
+            for p in range(Z):
+                came(q_buf.at[1, p], peer_r.at[p])
             each_group(turn_queries)
-        if s >= 1:
-            near(s - 1)
-        if s >= 2:
-            take_across(s - 2)
-        if s >= 3 and s % 2 == 1:
-            far(s - 3)
-    take_across(Z - 2)
-    near(Z - 1)
+        if s % 2 == 1:
+            gather([(0, s - 1), (1, s - 1), (0, s), (1, s)], s == 1)
+
+    def partial_sends():
+        return (
+            remote(blended_buf.at[1], other_blended, part_s.at[0], part_r.at[0], at(f, h, 1 - t)),
+            remote(stats.at[1], other_stats, part_s.at[1], part_r.at[1], at(f, h, 1 - t)),
+        )
+
+    def send_partial():
+        for c in partial_sends():
+            c.start()
 
     def o_send(s):
         return remote(o_out.at[s], o_buf.at[h], o_s.at[s], o_r.at[h], at(f - 1, lax.rem(h + Z - s, Z), t))
@@ -279,7 +263,12 @@
     def lo_send(s):
         return remote(o_out.at[s], lo_buf, o_s.at[s], lo_r, at(h, lax.rem(h + Z - s, Z), t))
 
-    def leave_with(blended, total, i):
+    def leave(i, carry):
+        mine, theirs = stats[0, 0, 0:1, columns(i)], other_stats[0, 0:1, columns(i)]
+        highest = jnp.maximum(mine, theirs)
+        mine, theirs = jnp.exp2((mine - highest) * rate), jnp.exp2((theirs - highest) * rate)
+        total = mine * stats[0, 1, 0:1, columns(i)] + theirs * other_stats[1, 0:1, columns(i)]
+        blended = mine * blended_buf[0, :, columns(i)] + theirs * other_blended[:, columns(i)]
         result = (blended / total).T.astype(jnp.bfloat16)
         for g in range(group):
             s = i * group + g
@@ -297,27 +286,22 @@
             def _():
                 pltpu.make_async_copy(o_out.at[0], lo_buf, lo_r).start()
 
+        return carry
+
     @pl.when(has_across)
     def _():
-        came(kv_buf.at[2, Z - 1, t], fr_r.at[1, Z - 1])
-        fwd_send(2, Z - 1).start()
-        wait_across(Z - 2)
-        keys, values = block_pair([(2, Z - 2), (2, Z - 1)])
-
-        def last(i, carry):
-            _, total, blended = merged(i, keys, values, False)
-            leave_with(blended, total, i)
-            return carry
-
-        each_group(last)
+        for s in range(1, Z, 2):
+            for p in (s - 1, s):
+                came(kv_buf.at[2, p], fr_r.at[1, p])
+            gather([(2, s - 1), (2, s)], False, send_partial if s == Z - 1 else None)
 
     @pl.when(jnp.logical_not(has_across))
     def _():
-        def last(i, carry):
-            leave_with(blended_buf[:, columns(i)], weight_sum[0:1, columns(i)], i)
-            return carry
-
-        each_group(last)
+        send_partial()
+
+    came(other_blended, part_r.at[0])
+    came(other_stats, part_r.at[1])
+    each_group(leave)
 
     came(lres_buf, lres_r)
     came(lgate_buf, lgate_r)
@@ -341,18 +325,14 @@
     def _():
         incoming.wait()
 
+    for c in partial_sends():
+        c.wait_send()
     for s in range(Z):
         if s > 0:
             kv_send(s).wait_send()
             q_send(s).wait_send()
-        peer_send(s, kv_out.at[0]).wait_send()
+        peer_send(s, q_out.at[0]).wait_send()
         pair_send(s, kv_out.at[0]).wait_send()
-        fwd_send(1, s).wait_send()
-
-        @pl.when(has_across)
-        def _():
-            fwd_send(2, s).wait_send()
-
         if relay:
 
             @pl.when(jnp.logical_not(has_across))
@@ -407,8 +387,8 @@
                 pltpu.VMEM((Z, 2, T, HD), bf),
                 pltpu.VMEM((Z, T, HD), bf),
                 pltpu.VMEM((8, HH), f32),
-                pltpu.VMEM((3, Z, 2, 2, T, HD), bf),
-                pltpu.VMEM((Z, T, HD), bf),
+                pltpu.VMEM((3, Z, 2, T, HD), bf),
+                pltpu.VMEM((2, Z, T, HD), bf),
                 pltpu.VMEM((Z, T, HD), bf),
                 pltpu.VMEM((Z, T, HD), bf),
                 pltpu.VMEM((T, HD), bf),
@@ -416,13 +396,14 @@
                 pltpu.VMEM((T, HD), bf),
                 pltpu.VMEM((8, HH), f32),
                 pltpu.VMEM((8, HD), f32),
-                pltpu.VMEM((HD, Z * T), bf),
-                pltpu.VMEM((8, Z * T), f32),
-                pltpu.VMEM((8, Z * T), f32),
+                pltpu.VMEM((2, HD, Z * T), bf),
+                pltpu.VMEM((2, 2, 8, Z * T), f32),
+                pltpu.VMEM((2, HD, Z * T), f32),
+                pltpu.VMEM((2, 8, Z * T), f32),
                 pltpu.VMEM((HD, Z * T), f32),
                 dma((3,)), dma((Z,)),
                 dma((Z,)), dma((Z,)), dma((Z,)), dma((Z,)),
-                dma((Z,)), dma((Z,)), dma((2, Z)), dma((2, Z)), dma((2, Z)), dma((2, Z)),
+                dma((Z,)), dma((Z,)), dma((2, Z)), dma((2, Z)), dma((2,)), dma((2,)),
                 dma((Z,)), dma((Z,)), dma,
                 dma, dma, dma((F,)), dma,
                 dma, dma, dma((F,)), dma,

time: 33.7 us -> 37.1 us (1.10)
  Pallas kernels: 30.3 us -> 33.8 us
    pallas_call x1, Pallas kernels: 30.3 us -> 33.8 us  [per_device(): pl.pallas_call(functools.partial(kernel, F, Z, F == 4), out_shape=(jax.Sh...]
where the time goes in v5:
time: 37.1 us; the launch traced here: 37 us
  Pallas kernels  33.8 us (91%)
  between operations  1.93 us (5%)
  local copies, waits for them, and re-layouts  1.25 us (3%)
    pallas_call x1, Pallas kernels, per_device(): pl.pallas_call(functools.partial(kernel, F, Z, F == 4), out_shape=(jax.Sh...  33.8 us
    unnamed x2, local copies, waits for them, and re-layouts  1.25 us

profile of v5, /device:TPU:0, one launch (start us, length us, event | category | flops | bytes accessed | tf_op | source)
XLA Modules:
  0.0 37.0 jit_solution(12783592119668877440)
XLA Ops:
  1.9 33.8 %shard_map.95 = (bf16[1,96,512]{2,1,0:T(8,128)(2,1)S(1)}, bf16[96,128]{1,0:T(8,128)(2,1)S(1)}) custom-call(bf16[1,96,512]{2,1,0:T(8,128)(2,1)} %q_hbm.1, bf16[1,96,512]{2,1,0:T(8,128)(2,1)} %k_hbm.1, bf16[1,96,512]{2,1,0:T(8,128)(2,1)} %v_hbm.1, bf16[1,96,512]{2,1,0:T(8,128)(2,1)} %res_hbm.1, bf16[96,512]{1,0:T(8,128)(2,1)} %inc_hbm.1, f32[50,512]{1,0:T(8,128)} %gate_hbm.1, ...), custom_call_target="tpu_custom_call" | custom-call | tf_op jit(solution)/shard_map/pallas_call | solution.py:375
  35.7 0.6 %copy.14 = bf16[1,96,512]{2,1,0:T(8,128)(2,1)} copy(bf16[1,96,512]{2,1,0:T(8,128)(2,1)S(1)} %get-tuple-element.4) | data formatting | bytes 196608
  36.4 0.6 %copy.15 = bf16[96,128]{1,0:T(8,128)(2,1)} copy(bf16[96,128]{1,0:T(8,128)(2,1)S(1)} %get-tuple-element.5) | data formatting | bytes 49152

commit v6 on v4

--- a/solution.py
+++ b/solution.py
@@ -19,7 +19,7 @@
     nq_ref, lv_ref,
     q_in, k_in, gate_in, kv_out, q_out, gate_out,
     kv_buf, q_buf, o_out, o_buf, lo_buf, res_buf, lres_buf, gate_buf, lgate_buf,
-    q_cols, top, weight_sum, blended_buf,
+    q_cols, top, weight_sum, blended_buf, q_relay, kv_relay,
     load_sem, v_sem, kvz_s, kvz_r, qz_s, qz_r, peer_s, peer_r, fr_s, fr_r, fwd_s, fwd_r,
     o_s, o_r, lo_r, res_s, res_r, lres_s, lres_r, gate_s, gate_r, lgate_s, lgate_r, out_sem,
 ):
@@ -93,17 +93,56 @@
         c.wait()
     pl.semaphore_wait(barrier, F * Z)
 
-    def q_send(s):
-        return remote(q_out.at[lax.rem(h + s, Z)], q_buf.at[s], qz_s.at[s], qz_r.at[s], at(f, lax.rem(h + s, Z), t))
-
-    def kv_send(s):
-        d = lax.rem(h + s, Z)
-        return remote(kv_out.at[d], kv_buf.at[0, s, t], kvz_s.at[s], kvz_r.at[s], at(f, d, t))
-
-    for s in range(1, Z):
-        q_send(s).start()
-    for s in range(1, Z):
-        kv_send(s).start()
+    hops = [(d, k) for k in range(Z - 1) for d in range(Z - 1, k, -1)]
+    spot = {pair: n for n, pair in enumerate(hops)}
+    both = (0, 1)
+
+    def runs(d, k, way, place):
+        return (place >= k) & (place - k + d < Z) if way == 0 else (place + k < Z) & (place + k >= d)
+
+    def comes(d, k, way):
+        return runs(d, k, way, h - 1) if way == 0 else runs(d, k, way, h + 1)
+
+    def slot_of(place, d, way):
+        nearer = jnp.minimum(place, d - 1) + jnp.minimum(Z - 1 - place, d - 1) + 1
+        return nearer if way == 0 else nearer + (place >= d).astype(jnp.int32)
+
+    def source_of(s):
+        source = h
+        for d in range(1, Z):
+            source = jnp.where((h >= d) & (slot_of(h, d, 0) == s), h - d, source)
+            source = jnp.where((h + d < Z) & (slot_of(h, d, 1) == s), h + d, source)
+        return source
+
+    def z_send(own, relayed, target, sems, d, k, way):
+        step = 1 - 2 * way
+        n = spot[d, k]
+        dst = h + step * (d - k)
+        block = own.at[dst] if k == 0 else relayed.at[way, spot[d, k - 1]]
+        landing = target(slot_of(h + step, d, way)) if k == d - 1 else relayed.at[way, n]
+        return remote(block, landing, sems[0].at[way, n], sems[1].at[way, n], at(f, h + step, t))
+
+    def q_target(s):
+        return q_buf.at[s]
+
+    def kv_target(s):
+        return kv_buf.at[0, s, t]
+
+    def q_send(d, k, way):
+        return z_send(q_out, q_relay, q_target, (qz_s, qz_r), d, k, way)
+
+    def kv_send(d, k, way):
+        return z_send(kv_out, kv_relay, kv_target, (kvz_s, kvz_r), d, k, way)
+
+    def when_runs(d, k, way, send):
+        @pl.when(runs(d, k, way, h))
+        def _():
+            send(d, k, way).start()
+
+    for send in (q_send, kv_send):
+        for d in range(Z - 1, 0, -1):
+            for way in both:
+                when_runs(d, 0, way, send)
 
     def peer_send(s, src):
         return remote(src, kv_buf.at[0, s, t], peer_s.at[s], peer_r.at[s], at(f, h, 1 - t))
@@ -143,9 +182,25 @@
     def came(ref, sem):
         remote(ref, ref, sem, sem, at(f, h, 1 - t)).wait_recv()
 
-    def take_own(s):
-        came(kv_buf.at[0, s, t], kvz_r.at[s])
-        spread(s, kv_buf.at[0, s, t])
+    def take(k, send, relayed, target, sem, arrived):
+        for d in range(Z - 1, k, -1):
+            for way in both:
+
+                @pl.when(comes(d, k, way))
+                def _():
+                    if k == d - 1:
+                        s = slot_of(h, d, way)
+                        came(target(s), sem.at[way, spot[d, k]])
+                        arrived(s)
+                    else:
+                        came(relayed.at[way, spot[d, k]], sem.at[way, spot[d, k]])
+                        send(d, k + 1, way).start()
+
+    def take_queries(k):
+        take(k, q_send, q_relay, q_target, qz_r, lambda s: None)
+
+    def take_own(k):
+        take(k, kv_send, kv_relay, kv_target, kvz_r, lambda s: spread(s, kv_buf.at[0, s, t]))
 
     def take_pair(s):
         came(kv_buf.at[1, s, t], fr_r.at[0, s])
@@ -254,15 +309,16 @@
             wait_across(s)
             gather([(2, s), (2, s + 1)], False)
 
+    take_queries(0)
     for s in range(Z):
+        if s + 2 < Z:
+            take_queries(s + 1)
         if s + 1 < Z:
-            take_own(s + 1)
+            take_own(s)
         take_pair(s)
         if s == Z - 1:
             send_residual()
         if s == 1:
-            for p in range(1, Z):
-                came(q_buf.at[p], qz_r.at[p])
             each_group(turn_queries)
         if s >= 1:
             near(s - 1)
@@ -274,10 +330,10 @@
     near(Z - 1)
 
     def o_send(s):
-        return remote(o_out.at[s], o_buf.at[h], o_s.at[s], o_r.at[h], at(f - 1, lax.rem(h + Z - s, Z), t))
+        return remote(o_out.at[s], o_buf.at[h], o_s.at[s], o_r.at[h], at(f - 1, source_of(s), t))
 
     def lo_send(s):
-        return remote(o_out.at[s], lo_buf, o_s.at[s], lo_r, at(h, lax.rem(h + Z - s, Z), t))
+        return remote(o_out.at[s], lo_buf, o_s.at[s], lo_r, at(h, source_of(s), t))
 
     def leave_with(blended, total, i):
         result = (blended / total).T.astype(jnp.bfloat16)
@@ -341,10 +397,15 @@
     def _():
         incoming.wait()
 
+    for d, k in hops:
+        for way in both:
+
+            @pl.when(runs(d, k, way, h))
+            def _():
+                q_send(d, k, way).wait_send()
+                kv_send(d, k, way).wait_send()
+
     for s in range(Z):
-        if s > 0:
-            kv_send(s).wait_send()
-            q_send(s).wait_send()
         peer_send(s, kv_out.at[0]).wait_send()
         pair_send(s, kv_out.at[0]).wait_send()
         fwd_send(1, s).wait_send()
@@ -388,6 +449,7 @@
         T, HH = queries.shape[1], queries.shape[2]
         assert HH == Z * HD and HH == F * HD and mesh.shape["tok"] == 2
         blocks = (queries, keys, values, residual, incoming, gate_table)
+        steps = Z * (Z - 1) // 2
         bf, f32 = jnp.bfloat16, jnp.float32
         dma = pltpu.SemaphoreType.DMA
         anywhere = pl.BlockSpec(memory_space=pl.ANY)
@@ -420,8 +482,10 @@
                 pltpu.VMEM((8, Z * T), f32),
                 pltpu.VMEM((8, Z * T), f32),
                 pltpu.VMEM((HD, Z * T), f32),
+                pltpu.VMEM((2, steps, T, HD), bf),
+                pltpu.VMEM((2, steps, 2, T, HD), bf),
                 dma((3,)), dma((Z,)),
-                dma((Z,)), dma((Z,)), dma((Z,)), dma((Z,)),
+                dma((2, steps)), dma((2, steps)), dma((2, steps)), dma((2, steps)),
                 dma((Z,)), dma((Z,)), dma((2, Z)), dma((2, Z)), dma((2, Z)), dma((2, Z)),
                 dma((Z,)), dma((Z,)), dma,
                 dma, dma, dma((F,)), dma,

time: 33.7 us -> 36.4 us (1.080)
  Pallas kernels: 30.3 us -> 33.1 us
    pallas_call x1, Pallas kernels: 30.3 us -> 33.1 us  [per_device(): pl.pallas_call(functools.partial(kernel, F, Z, F == 4), out_shape=(jax.Sh...]
where the time goes in v6:
time: 36.4 us; the launch traced here: 36.3 us
  Pallas kernels  33.1 us (91%)
  between operations  1.93 us (5%)
  local copies, waits for them, and re-layouts  1.25 us (3%)
    pallas_call x1, Pallas kernels, per_device(): pl.pallas_call(functools.partial(kernel, F, Z, F == 4), out_shape=(jax.Sh...  33.1 us
    unnamed x2, local copies, waits for them, and re-layouts  1.25 us

profile of v6, /device:TPU:0, one launch (start us, length us, event | category | flops | bytes accessed | tf_op | source)
XLA Modules:
  0.0 36.3 jit_solution(15424296774854385708)
XLA Ops:
  1.9 33.1 %shard_map.95 = (bf16[1,96,512]{2,1,0:T(8,128)(2,1)S(1)}, bf16[96,128]{1,0:T(8,128)(2,1)S(1)}) custom-call(bf16[1,96,512]{2,1,0:T(8,128)(2,1)} %q_hbm.1, bf16[1,96,512]{2,1,0:T(8,128)(2,1)} %k_hbm.1, bf16[1,96,512]{2,1,0:T(8,128)(2,1)} %v_hbm.1, bf16[1,96,512]{2,1,0:T(8,128)(2,1)} %res_hbm.1, bf16[96,512]{1,0:T(8,128)(2,1)} %inc_hbm.1, f32[50,512]{1,0:T(8,128)} %gate_hbm.1, ...), custom_call_target="tpu_custom_call" | custom-call | tf_op jit(solution)/shard_map/pallas_call | solution.py:457
  35.0 0.6 %copy.14 = bf16[1,96,512]{2,1,0:T(8,128)(2,1)} copy(bf16[1,96,512]{2,1,0:T(8,128)(2,1)S(1)} %get-tuple-element.4) | data formatting | bytes 196608
  35.7 0.6 %copy.15 = bf16[96,128]{1,0:T(8,128)(2,1)} copy(bf16[96,128]{1,0:T(8,128)(2,1)S(1)} %get-tuple-element.5) | data formatting | bytes 49152

commit v7 on v2

--- a/solution.py
+++ b/solution.py
@@ -18,7 +18,7 @@
     q_hbm, k_hbm, v_hbm, res_hbm, inc_hbm, gate_hbm, steps_ref, pos_ref,
     nq_ref, lv_ref,
     q_in, k_in, gate_in, kv_out, q_out, gate_out,
-    kv_buf, q_buf, o_out, o_buf, lo_buf, res_buf, lres_buf, gate_buf, lgate_buf, nq_buf, lv_buf,
+    kv_buf, q_buf, o_out, o_buf, lo_buf, res_buf, lres_buf, gate_buf, lgate_buf,
     top, weight_sum, blended_buf,
     load_sem, v_sem, kvz_s, kvz_r, qz_s, qz_r, peer_s, peer_r, fr_s, fr_r, fwd_s, fwd_r,
     o_s, o_r, lo_r, res_s, res_r, lres_s, lres_r, gate_s, gate_r, lgate_s, lgate_r, out_sem,
@@ -47,11 +47,16 @@
     load_v = [
         pltpu.make_async_copy(v_hbm.at[0, :, pl.ds(j * HD, HD)], kv_out.at[j, 1], v_sem.at[j]) for j in range(Z)
     ]
+    incoming = pltpu.make_async_copy(inc_hbm, nq_ref.at[0], out_sem)
     load_k.start()
     for c in load_v:
         c.start()
     load_q.start()
     load_gate.start()
+
+    @pl.when(f == F - 1)
+    def _():
+        incoming.start()
 
     barrier = pltpu.get_barrier_semaphore()
     me = f * Z + h
@@ -81,9 +86,6 @@
     load_k.wait()
     for j in range(Z):
         kv_out[j, 0] = turned(k_in[:, j * HD : (j + 1) * HD])
-    load_q.wait()
-    for j in range(Z):
-        q_out[j] = turned(q_in[:, j * HD : (j + 1) * HD])
     for c in load_v:
         c.wait()
     pl.semaphore_wait(barrier, F * Z)
@@ -128,6 +130,9 @@
         peer_send(s, b, src).start()
 
     spread(0, h, kv_out.at[h])
+    load_q.wait()
+    for j in range(Z):
+        q_out[j] = turned(q_in[:, j * HD : (j + 1) * HD])
     for s in range(1, Z):
         q_send(s).start()
     kv_buf[0, t, h] = kv_out[h]
@@ -139,21 +144,28 @@
     def came(ref, sem):
         remote(ref, ref, sem, sem, at(f, h, 1 - t)).wait_recv()
 
-    for s in range(1, Z):
-        b = lax.rem(h + Z - s, Z)
-        came(kv_buf.at[0, t, b], kvz_r.at[s])
-        spread(s, b, kv_buf.at[0, t, b])
-
-    for s in range(Z):
-        b = lax.rem(h + Z - s, Z)
-        came(kv_buf.at[1, t, b], fr_r.at[0, s])
+    def block(s):
+        return lax.rem(h + Z - s, Z)
+
+    def take_own(s):
+        came(kv_buf.at[0, t, block(s)], kvz_r.at[s])
+        spread(s, block(s), kv_buf.at[0, t, block(s)])
+
+    def take_pair(s):
+        came(kv_buf.at[1, t, block(s)], fr_r.at[0, s])
         if relay:
 
             @pl.when(jnp.logical_not(has_across))
             def _():
-                relay_send(s, b).start()
-
-        fwd_send(1, s, b).start()
+                relay_send(s, block(s)).start()
+
+        fwd_send(1, s, block(s)).start()
+
+    def take_across(s):
+        @pl.when(has_across)
+        def _():
+            came(kv_buf.at[2, t, block(s)], fr_r.at[1, s])
+            fwd_send(2, s, block(s)).start()
 
     def res_send():
         return remote(res_hbm, res_buf, res_s, res_r, at(f - 1, h, t))
@@ -167,18 +179,28 @@
     def lgate_send(g):
         return remote(gate_out.at[:, pl.ds(g * HD, HD)], lgate_buf, lgate_s.at[g], lgate_r, at(g, h, t))
 
-    @pl.when(has_prev)
-    def _():
-        res_send().start()
-        gate_send().start()
-
-    @pl.when(f == 0)
-    def _():
-        pltpu.make_async_copy(res_hbm.at[0, :, pl.ds(0, HD)], lres_buf, lres_r).start()
-        pltpu.make_async_copy(gate_out.at[:, pl.ds(0, HD)], lgate_buf, lgate_r).start()
-        for g in range(1, F):
-            lres_send(g).start()
-            lgate_send(g).start()
+    def send_residual():
+        @pl.when(has_prev)
+        def _():
+            res_send().start()
+            gate_send().start()
+
+        @pl.when(f == 0)
+        def _():
+            pltpu.make_async_copy(res_hbm.at[0, :, pl.ds(0, HD)], lres_buf, lres_r).start()
+            pltpu.make_async_copy(gate_out.at[:, pl.ds(0, HD)], lgate_buf, lgate_r).start()
+            for g in range(1, F):
+                lres_send(g).start()
+                lgate_send(g).start()
+
+    for s in range(Z):
+        take_pair(s)
+        if s + 1 < Z:
+            take_own(s + 1)
+        if s == Z - 2:
+            send_residual()
+        if s >= 1:
+            take_across(s - 1)
 
     for s in range(Z):
         b = lax.rem(h + s, Z)
@@ -220,26 +242,17 @@
         weight_sum[at_rows] = jnp.broadcast_to(total, (group * T, HD))
         blended_buf[at_rows] = blend(own, 0) + blend(beside, 1)
 
-    if Z <= 4:
-        for i in range(Z // group):
-            for s in range(max(i * group, 1), (i + 1) * group):
-                came(q_buf.at[s], qz_r.at[s])
-            near(i, i == 0)
-    else:
-        for s in range(1, Z):
+    def take_queries(i):
+        for s in range(max(i * group, 1), (i + 1) * group):
             came(q_buf.at[s], qz_r.at[s])
-        near(0, True)
-        lax.fori_loop(1, Z // group, lambda i, c: (near(i, False), c)[1], 0)
-
-    @pl.when(has_across)
-    def _():
-        for s in range(Z):
-            b = lax.rem(h + Z - s, Z)
-            came(kv_buf.at[2, t, b], fr_r.at[1, s])
-            fwd_send(2, s, b).start()
-        for s in range(Z):
-            b = lax.rem(h + Z - s, Z)
-            came(kv_buf.at[2, 1 - t, b], fwd_r.at[1, s])
+
+    def finish_across():
+        take_across(Z - 1)
+
+        @pl.when(has_across)
+        def _():
+            for s in range(Z):
+                came(kv_buf.at[2, 1 - t, block(s)], fwd_r.at[1, s])
 
     def o_send(s):
         return remote(o_out.at[s], o_buf.at[h], o_s.at[s], o_r.at[h], at(f - 1, lax.rem(h + Z - s, Z), t))
@@ -285,34 +298,40 @@
 
     if Z <= 4:
         for i in range(Z // group):
+            take_queries(i)
+            near(i, i == 0)
+            if i == 0:
+                finish_across()
             finish(i, 0)
     else:
+        for i in range(Z // group):
+            take_queries(i)
+        near(0, True)
+        finish_across()
+        lax.fori_loop(1, Z // group, lambda i, c: (near(i, False), c)[1], 0)
         lax.fori_loop(0, Z // group, finish, 0)
+
+    came(lres_buf, lres_r)
+    came(lgate_buf, lgate_r)
+    came(lo_buf, lo_r)
+    lv_ref[...] = (
+        lres_buf[...].astype(jnp.float32) + lgate_buf[0:1, :] * lo_buf[...].astype(jnp.float32)
+    ).astype(jnp.bfloat16)
+
+    @pl.when(f < F - 1)
+    def _():
+        came(res_buf, res_r)
+        came(gate_buf, gate_r)
+        for j in range(Z):
+            came(o_buf.at[j], o_r.at[j])
+            cols = slice(j * HD, (j + 1) * HD)
+            nq_ref[0, :, cols] = (
+                res_buf[0, :, cols].astype(jnp.float32) + gate_buf[0:1, cols] * o_buf[j].astype(jnp.float32)
+            ).astype(jnp.bfloat16)
 
     @pl.when(f == F - 1)
     def _():
-        pltpu.make_async_copy(inc_hbm, nq_ref.at[0], out_sem.at[0]).start()
-
-    @pl.when(f < F - 1)
-    def _():
-        remote(res_hbm, res_buf, res_s, res_r, at(f, h, 1 - t)).wait_recv()
-        remote(gate_out, gate_buf, gate_s, gate_r, at(f, h, 1 - t)).wait_recv()
-        for j in range(Z):
-            remote(o_out.at[0], o_buf.at[j], o_s.at[0], o_r.at[j], at(f, h, 1 - t)).wait_recv()
-            cols = slice(j * HD, (j + 1) * HD)
-            nq_buf[:, cols] = (
-                res_buf[0, :, cols].astype(jnp.float32) + gate_buf[0:1, cols] * o_buf[j].astype(jnp.float32)
-            ).astype(jnp.bfloat16)
-        pltpu.make_async_copy(nq_buf, nq_ref.at[0], out_sem.at[0]).start()
-
-    remote(lres_buf, lres_buf, lres_s.at[0], lres_r, at(f, h, 1 - t)).wait_recv()
-    remote(lgate_buf, lgate_buf, lgate_s.at[0], lgate_r, at(f, h, 1 - t)).wait_recv()
-    remote(lo_buf, lo_buf, o_s.at[0], lo_r, at(f, h, 1 - t)).wait_recv()
-    lv_buf[...] = (
-        lres_buf[...].astype(jnp.float32) + lgate_buf[0:1, :] * lo_buf[...].astype(jnp.float32)
-    ).astype(jnp.bfloat16)
-    leave = pltpu.make_async_copy(lv_buf, lv_ref, out_sem.at[1])
-    leave.start()
+        incoming.wait()
 
     for s in range(Z):
         if s > 0:
@@ -353,9 +372,6 @@
             lres_send(g).wait_send()
             lgate_send(g).wait_send()
 
-    pltpu.make_async_copy(inc_hbm, nq_ref.at[0], out_sem.at[0]).wait()
-    leave.wait()
-
 
 def solution(mesh):
     F, Z = mesh.shape["frame"], mesh.shape["head"]
@@ -363,6 +379,7 @@
     def per_device(queries, keys, values, residual, incoming, gate_table, timesteps, positions):
         T, HH = queries.shape[1], queries.shape[2]
         assert HH == Z * HD and HH == F * HD and mesh.shape["tok"] == 2
+        blocks = (queries, keys, values, residual, incoming, gate_table)
         bf, f32 = jnp.bfloat16, jnp.float32
         dma = pltpu.SemaphoreType.DMA
         anywhere = pl.BlockSpec(memory_space=pl.ANY)
@@ -374,7 +391,7 @@
                 jax.ShapeDtypeStruct((T, HD), bf),
             ),
             in_specs=[anywhere] * 6 + [smem, smem],
-            out_specs=(anywhere, anywhere),
+            out_specs=(pl.BlockSpec(memory_space=pltpu.VMEM),) * 2,
             scratch_shapes=[
                 pltpu.VMEM((T, HH), bf),
                 pltpu.VMEM((T, HH), bf),
@@ -391,8 +408,6 @@
                 pltpu.VMEM((T, HD), bf),
                 pltpu.VMEM((8, HH), f32),
                 pltpu.VMEM((8, HD), f32),
-                pltpu.VMEM((T, HH), bf),
-                pltpu.VMEM((T, HD), bf),
                 pltpu.VMEM((Z * T, HD), f32),
                 pltpu.VMEM((Z * T, HD), f32),
                 pltpu.VMEM((Z * T, HD), f32),
@@ -402,12 +417,14 @@
                 dma((Z,)), dma((Z,)), dma,
                 dma, dma, dma((F,)), dma,
                 dma, dma, dma((F,)), dma,
-                dma((2,)),
+                dma,
             ],
             compiler_params=pltpu.CompilerParams(
-                collective_id=0, has_side_effects=True, vmem_limit_bytes=60 * 1024 * 1024
+                collective_id=0, has_side_effects=True, vmem_limit_bytes=48 * 1024 * 1024
             ),
-        )(queries, keys, values, residual, incoming, gate_table, timesteps, positions)
+        )(
+            *(pltpu.with_memory_space_constraint(x, pltpu.HBM) for x in blocks), timesteps, positions
+        )
 
     placed = (
         P("frame", ("head", "tok"), None),

time: 33.2 us -> 34.5 us (1.039)
  Pallas kernels: 28.9 us -> 31.1 us
  local copies, waits for them, and re-layouts: 2.16 us -> 1.25 us
    pallas_call x1, Pallas kernels: 28.9 us -> 31.1 us  [per_device(): pl.pallas_call(functools.partial(kernel, F, Z, F == 4), out_shape=(jax.Sh...]
    unnamed x4 -> x2, local copies, waits for them, and re-layouts: 2.16 us -> 1.25 us
where the time goes in v7:
time: 34.5 us; the launch traced here: 34.3 us
  Pallas kernels  31.1 us (90%)
  between operations  1.93 us (6%)
  local copies, waits for them, and re-layouts  1.25 us (4%)
    pallas_call x1, Pallas kernels, per_device(): pl.pallas_call(functools.partial(kernel, F, Z, F == 4), out_shape=(jax.Sh...  31.1 us
    unnamed x2, local copies, waits for them, and re-layouts  1.25 us

profile of v7, /device:TPU:0, one launch (start us, length us, event | category | flops | bytes accessed | tf_op | source)
XLA Modules:
  0.0 34.3 jit_solution(12546332544964116355)
XLA Ops:
  1.9 31.1 %shard_map.95 = (bf16[1,96,512]{2,1,0:T(8,128)(2,1)S(1)}, bf16[96,128]{1,0:T(8,128)(2,1)S(1)}) custom-call(bf16[1,96,512]{2,1,0:T(8,128)(2,1)} %q_hbm.1, bf16[1,96,512]{2,1,0:T(8,128)(2,1)} %k_hbm.1, bf16[1,96,512]{2,1,0:T(8,128)(2,1)} %v_hbm.1, bf16[1,96,512]{2,1,0:T(8,128)(2,1)} %res_hbm.1, bf16[96,512]{1,0:T(8,128)(2,1)} %inc_hbm.1, f32[50,512]{1,0:T(8,128)} %gate_hbm.1, ...), custom_call_target="tpu_custom_call" | custom-call | tf_op jit(solution)/shard_map/pallas_call | solution.py:387
  33.1 0.6 %copy.14 = bf16[1,96,512]{2,1,0:T(8,128)(2,1)} copy(bf16[1,96,512]{2,1,0:T(8,128)(2,1)S(1)} %get-tuple-element.4) | data formatting | bytes 196608
  33.7 0.6 %copy.15 = bf16[96,128]{1,0:T(8,128)(2,1)} copy(bf16[96,128]{1,0:T(8,128)(2,1)S(1)} %get-tuple-element.5) | data formatting | bytes 49152

commit v8 on v7

--- a/solution.py
+++ b/solution.py
@@ -193,14 +193,11 @@
                 lres_send(g).start()
                 lgate_send(g).start()
 
+    for s in range(1, Z):
+        take_own(s)
     for s in range(Z):
         take_pair(s)
-        if s + 1 < Z:
-            take_own(s + 1)
-        if s == Z - 2:
-            send_residual()
-        if s >= 1:
-            take_across(s - 1)
+    send_residual()
 
     for s in range(Z):
         b = lax.rem(h + s, Z)
@@ -247,7 +244,8 @@
             came(q_buf.at[s], qz_r.at[s])
 
     def finish_across():
-        take_across(Z - 1)
+        for s in range(Z):
+            take_across(s)
 
         @pl.when(has_across)
         def _():
@@ -300,8 +298,8 @@
         for i in range(Z // group):
             take_queries(i)
             near(i, i == 0)
-            if i == 0:
-                finish_across()
+        finish_across()
+        for i in range(Z // group):
             finish(i, 0)
     else:
         for i in range(Z // group):

time: 34.5 us -> 31.7 us (0.919)
  Pallas kernels: 31.1 us -> 28.3 us
    pallas_call x1, Pallas kernels: 31.1 us -> 28.3 us  [per_device(): pl.pallas_call(functools.partial(kernel, F, Z, F == 4), out_shape=(jax.Sh...]
where the time goes in v8:
time: 31.7 us; the launch traced here: 31.5 us
  Pallas kernels  28.3 us (89%)
  between operations  1.93 us (6%)
  local copies, waits for them, and re-layouts  1.25 us (4%)
    pallas_call x1, Pallas kernels, per_device(): pl.pallas_call(functools.partial(kernel, F, Z, F == 4), out_shape=(jax.Sh...  28.3 us
    unnamed x2, local copies, waits for them, and re-layouts  1.25 us

profile of v8, /device:TPU:0, one launch (start us, length us, event | category | flops | bytes accessed | tf_op | source)
XLA Modules:
  0.0 31.5 jit_solution(16735536652313829452)
XLA Ops:
  1.9 28.3 %shard_map.95 = (bf16[1,96,512]{2,1,0:T(8,128)(2,1)S(1)}, bf16[96,128]{1,0:T(8,128)(2,1)S(1)}) custom-call(bf16[1,96,512]{2,1,0:T(8,128)(2,1)} %q_hbm.1, bf16[1,96,512]{2,1,0:T(8,128)(2,1)} %k_hbm.1, bf16[1,96,512]{2,1,0:T(8,128)(2,1)} %v_hbm.1, bf16[1,96,512]{2,1,0:T(8,128)(2,1)} %res_hbm.1, bf16[96,512]{1,0:T(8,128)(2,1)} %inc_hbm.1, f32[50,512]{1,0:T(8,128)} %gate_hbm.1, ...), custom_call_target="tpu_custom_call" | custom-call | tf_op jit(solution)/shard_map/pallas_call | solution.py:385
  30.2 0.6 %copy.14 = bf16[1,96,512]{2,1,0:T(8,128)(2,1)} copy(bf16[1,96,512]{2,1,0:T(8,128)(2,1)S(1)} %get-tuple-element.4) | data formatting | bytes 196608
  30.9 0.6 %copy.15 = bf16[96,128]{1,0:T(8,128)(2,1)} copy(bf16[96,128]{1,0:T(8,128)(2,1)S(1)} %get-tuple-element.5) | data formatting | bytes 49152

commit v9 on v8

--- a/solution.py
+++ b/solution.py
@@ -195,8 +195,8 @@
 
     for s in range(1, Z):
         take_own(s)
-    for s in range(Z):
-        take_pair(s)
+        take_pair(s - 1)
+    take_pair(Z - 1)
     send_residual()
 
     for s in range(Z):

time: 31.7 us -> 31.7 us (level)
  no operation moved by 1% of the time
where the time goes in v9:
time: 31.7 us; the launch traced here: 31.5 us
  Pallas kernels  28.3 us (89%)
  between operations  1.93 us (6%)
  local copies, waits for them, and re-layouts  1.25 us (4%)
    pallas_call x1, Pallas kernels, per_device(): pl.pallas_call(functools.partial(kernel, F, Z, F == 4), out_shape=(jax.Sh...  28.3 us
    unnamed x2, local copies, waits for them, and re-layouts  1.25 us

profile of v9, /device:TPU:0, one launch (start us, length us, event | category | flops | bytes accessed | tf_op | source)
XLA Modules:
  0.0 31.5 jit_solution(16696053128563574711)
XLA Ops:
  1.9 28.3 %shard_map.95 = (bf16[1,96,512]{2,1,0:T(8,128)(2,1)S(1)}, bf16[96,128]{1,0:T(8,128)(2,1)S(1)}) custom-call(bf16[1,96,512]{2,1,0:T(8,128)(2,1)} %q_hbm.1, bf16[1,96,512]{2,1,0:T(8,128)(2,1)} %k_hbm.1, bf16[1,96,512]{2,1,0:T(8,128)(2,1)} %v_hbm.1, bf16[1,96,512]{2,1,0:T(8,128)(2,1)} %res_hbm.1, bf16[96,512]{1,0:T(8,128)(2,1)} %inc_hbm.1, f32[50,512]{1,0:T(8,128)} %gate_hbm.1, ...), custom_call_target="tpu_custom_call" | custom-call | tf_op jit(solution)/shard_map/pallas_call | solution.py:385
  30.2 0.6 %copy.14 = bf16[1,96,512]{2,1,0:T(8,128)(2,1)} copy(bf16[1,96,512]{2,1,0:T(8,128)(2,1)S(1)} %get-tuple-element.4) | data formatting | bytes 196608
  30.9 0.6 %copy.15 = bf16[96,128]{1,0:T(8,128)(2,1)} copy(bf16[96,128]{1,0:T(8,128)(2,1)S(1)} %get-tuple-element.5) | data formatting | bytes 49152
